TPU v7x, 32 devices: a whole 2x2x4 slice. The times are simulated.
32 devices in a mesh: lat: 4 (over z), lon: 8 (over y, x, core).
Axes of the slice: x: 2, y: 2, z: 4, core: 2. Of those that a mesh axis runs over, the one named last changes fastest.
Arguments:
- control: float32 [4, 90, 32, 1024], P(None, None, 'lat', 'lon'), may hold values from -6 to 6
- kappa: float32 [4, 90, 32, 1024], P(None, None, 'lat', 'lon'), may hold values from 0.25 to 0.5
- pc_obs: bfloat16 [1024, 128, 300], P(('lat', 'lon')), may hold values from -6 to 6
- owner: int32 [1024, 1], P(('lat', 'lon')), may hold values from 0 to 31; in each aligned block of 32 rows (0 to 31, 32 to 63, ...) at most 2 rows name the same one
- columns: int32 [1024, 128], P(('lat', 'lon')), may hold values from 0 to 1023
- counts: int32 [1024], P(('lat', 'lon')), may hold values from 1 to 128, as said below
- jacobian: bfloat16 [360, 300], replicated, may hold values from -0.3125 to 0.3125
- obs_weight: float32 [300], replicated, may hold values from 0.3 to 3
Outputs:
- gradient: float32 [4, 90, 32, 1024], P(None, None, 'lat', 'lon')
Inputs may be any that keep to these rules, and one draw needn't show every extreme that they name: Among the 32 blocks of one device no owner is named more than 2 times, a bound that some block reaches. `counts`: the first block of every device is full.
All inputs are finite; a program needn't handle non-finite values.
Results may differ from a plain program's by a relative error of at most 0.0017.
Values may be sent and summed in bfloat16 or wider, within the bound.
A program may use at most 256 MiB of HBM per device.

v0:
```python
import jax
import jax.numpy as jnp
from jax import lax
from jax.experimental import pallas as pl
from jax.experimental.pallas import tpu as pltpu
from jax.sharding import PartitionSpec as P

CAP = 2
STEPS = 4
GROUP = 4


def ring(axis, step):
    count = lax.axis_size(axis)
    return [(i, (i + step) % count) for i in range(count)]


def rims(core, closed):
    north = lax.ppermute(core[:, -STEPS:], "lat", ring("lat", 1))
    south = lax.ppermute(core[:, :STEPS], "lat", ring("lat", -1))
    if closed:
        place = lax.axis_index("lat")
        zero = jnp.zeros((), core.dtype)
        north = jnp.where(place == 0, zero, north)
        south = jnp.where(place == lax.axis_size("lat") - 1, zero, south)
    main = jnp.concatenate([core, south, north], axis=1)
    planes = main.shape[0]
    head = main[:, :, :STEPS].reshape(planes, -1)
    tail = main[:, :, -STEPS:].reshape(planes, -1)
    west = lax.ppermute(tail, "lon", ring("lon", 1))
    east = lax.ppermute(head, "lon", ring("lon", -1))
    return main, jnp.concatenate([east, west], axis=1)


def side_tile(side, rows, width):
    planes = side.shape[0]
    parts = side.reshape(planes, 2, rows, STEPS)
    gap = jnp.zeros((planes, rows, width - 2 * STEPS), side.dtype)
    return jnp.concatenate([parts[:, 0], gap, parts[:, 1]], axis=2)


def spread_kernel(field_ref, side_ref, coef_ref, coef_side_ref, *refs):
    out_ref = refs[-1]
    core, width = out_ref.shape[1:]
    rows, lanes = field_ref.shape[1], 2 * width

    @pl.loop(0, out_ref.shape[0], unroll=4)
    def _(i):
        coef = jnp.concatenate([coef_ref[i], coef_side_ref[i]], axis=1)
        field = jnp.concatenate([field_ref[i], side_ref[i]], axis=1)
        south = coef * pltpu.roll(coef, rows - 1, 0)
        east = coef * pltpu.roll(coef, lanes - 1, 1)
        for repeat in range(STEPS):
            down = south * (pltpu.roll(field, rows - 1, 0) - field)
            along = east * (pltpu.roll(field, lanes - 1, 1) - field)
            field = field + (down - pltpu.roll(down, 1, 0)) + (along - pltpu.roll(along, 1, 1))
        result = field[:core, :width]
        out_ref[i] = result + refs[0][i] if len(refs) > 1 else result


def spread(field, side, coef, coef_side, core, *base):
    planes, rows, width = field.shape
    batch = max(n for n in range(4, 41, 4) if planes % n == 0)
    wide = pl.BlockSpec((batch, rows, width), lambda i: (i, 0, 0))
    thin = pl.BlockSpec((batch, core, width), lambda i: (i, 0, 0))
    return pl.pallas_call(
        spread_kernel,
        out_shape=jax.ShapeDtypeStruct((planes, core, width), jnp.float32),
        grid=(planes // batch,),
        in_specs=[wide] * 4 + [thin] * len(base),
        out_specs=thin,
        cost_estimate=pl.CostEstimate(
            flops=planes * rows * width * 80, bytes_accessed=planes * rows * width * 20, transcendentals=0
        ),
    )(field, side, coef, coef_side, *base)


def pack_kernel(source_ref, *refs):
    blocks, (code_ref, out_ref, wide) = refs[:CAP], refs[CAP:]
    comps = blocks[0].shape[2]
    for k, block in enumerate(blocks):
        wide[0:comps, :] = jnp.transpose(block[0].astype(jnp.float32))
        code = code_ref[0, k : k + 1, :]
        low = jnp.bitwise_and(code, 31)
        wide[comps : comps + 1, :] = jnp.ones((1, wide.shape[1]), jnp.float32)
        wide[comps + 1 : comps + 2, :] = jnp.right_shift(code - low, 5).astype(jnp.float32)
        wide[comps + 2 : comps + 3, :] = low.astype(jnp.float32)
        wide[comps + 3 :, :] = jnp.zeros((wide.shape[0] - comps - 3, wide.shape[1]), jnp.float32)
        out_ref[k] = wide[...].astype(jnp.bfloat16)


def pack(pc_obs, source, code, height):
    blocks, soundings, comps = pc_obs.shape
    slots = code.shape[0]

    def place(k):
        return lambda i, src: (src[i * CAP + k], 0, 0)

    return pl.pallas_call(
        pack_kernel,
        out_shape=jax.ShapeDtypeStruct((slots, height, soundings), jnp.bfloat16),
        grid_spec=pltpu.PrefetchScalarGridSpec(
            num_scalar_prefetch=1,
            grid=(slots // CAP,),
            in_specs=[pl.BlockSpec((1, soundings, comps), place(k)) for k in range(CAP)]
            + [pl.BlockSpec((1, CAP, soundings), lambda i, src: (i, 0, 0))],
            out_specs=pl.BlockSpec((CAP, height, soundings), lambda i, src: (i, 0, 0)),
            scratch_shapes=[pltpu.VMEM((height, soundings), jnp.float32)],
        ),
    )(source, *([pc_obs] * CAP), code.reshape(slots // CAP, CAP, soundings))


def gather_kernel(comps, got_ref, sums_ref):
    height, cells = sums_ref.shape

    @pl.when(pl.program_id(0) == 0)
    def _():
        sums_ref[...] = jnp.zeros_like(sums_ref)

    base = height - 16
    lines = []
    for k in range(GROUP):
        tail = got_ref[k, base:height, :].astype(jnp.float32)
        high = tail[comps + 1 - base : comps + 2 - base, :]
        lines.append((high * 32.0 + tail[comps + 2 - base : comps + 3 - base, :]).astype(jnp.int32))
    code = jnp.concatenate(lines, axis=1)
    cell = lax.broadcasted_iota(jnp.int32, (cells, code.shape[1]), 0)
    hot = jnp.where(cell == code, 1.0, 0.0).astype(jnp.bfloat16)
    obs = jnp.concatenate([got_ref[k] for k in range(GROUP)], axis=1)
    sums_ref[...] += lax.dot_general(
        obs, hot, (((1,), (1,)), ((), ())), preferred_element_type=jnp.float32
    )


def column_sums(got, comps, cells):
    slots, height, soundings = got.shape
    return pl.pallas_call(
        lambda *refs: gather_kernel(comps, *refs),
        out_shape=jax.ShapeDtypeStruct((height, cells), jnp.float32),
        grid=(slots // GROUP,),
        in_specs=[pl.BlockSpec((GROUP, height, soundings), lambda i: (i, 0, 0))],
        out_specs=pl.BlockSpec((height, cells), lambda i: (0, 0)),
        compiler_params=pltpu.CompilerParams(vmem_limit_bytes=32 * 2**20),
    )(got)


def per_device(control, kappa, pc_obs, owner, columns, counts, jacobian, obs_weight):
    peers = lax.axis_size("lat") * lax.axis_size("lon")
    fields, levels, rows, width_dev = control.shape
    blocks, soundings, comps = pc_obs.shape
    cells = rows * width_dev
    height = -(-(comps + 3) // 16) * 16
    slots = peers * CAP
    target = owner[:, 0]
    index = jnp.arange(blocks, dtype=jnp.int32)
    same = (target[:, None] == target[None, :]) & (index[None, :] < index[:, None])
    position = target * CAP + jnp.sum(same.astype(jnp.int32), axis=1)
    hits = position[None, :] == jnp.arange(slots, dtype=jnp.int32)[:, None]
    source = jnp.sum(jnp.where(hits, index[None, :], 0), axis=1)
    order = jnp.arange(soundings, dtype=jnp.int32)
    code = jnp.where(order[None, :] < counts[:, None], columns, -32)
    code = -32 + jnp.sum(jnp.where(hits[:, :, None], code[None] + 32, 0), axis=1)
    sent = pack(pc_obs, source, code, height)
    got = lax.all_to_all(sent, ("lat", "lon"), split_axis=0, concat_axis=0, tiled=True)

    planes = fields * levels
    extent = rows + 2 * STEPS
    start = control.reshape(planes, rows, width_dev)
    field, side = rims(start, False)
    coef, coef_side = rims(kappa.reshape(planes, rows, width_dev), True)
    coef_side = side_tile(coef_side, extent, width_dev)
    state = spread(field, side_tile(side, extent, width_dev), coef, coef_side, rows)
    table = state.astype(jnp.bfloat16).reshape(planes, cells)
    model = lax.dot_general(
        jacobian, table, (((0,), (0,)), ((), ())), preferred_element_type=jnp.float32
    )
    sums = column_sums(got, comps, cells)
    total = (sums[comps : comps + 1] * model - sums[:comps]) * obs_weight[:, None]
    total = total.astype(jnp.bfloat16).reshape(comps, rows, width_dev)
    total, total_side = rims(total, False)
    back, back_side = (
        lax.dot_general(
            jacobian, part.reshape(comps, -1), (((1,), (0,)), ((), ())), preferred_element_type=jnp.float32
        )
        for part in (total, total_side)
    )
    back = back.reshape(planes, extent, width_dev)
    result = spread(back, side_tile(back_side, extent, width_dev), coef, coef_side, rows, start)
    return result.reshape(control.shape)


def solution(mesh):
    placed = (
        P(None, None, "lat", "lon"),
        P(None, None, "lat", "lon"),
        P(("lat", "lon"), None, None),
        P(("lat", "lon"), None),
        P(("lat", "lon"), None),
        P(("lat", "lon")),
        P(),
        P(),
    )
    return jax.shard_map(
        per_device,
        mesh=mesh,
        in_specs=placed,
        out_specs=P(None, None, "lat", "lon"),
        check_vma=False,
    )
```

profile of v0, /device:TPU:0, one launch (start us, length us, event | category | flops | bytes accessed | tf_op | source)
XLA Modules:
  0.0 407.4 jit_solution(7811534318150141407)
XLA Ops:
  0.0 0.9 convert_reduce_fusion
  0.9 0.7 multiply_add_fusion
  1.7 0.7 select_reduce_fusion.1.source_ref
  2.3 0.1 copy.27
  2.4 0.8 select_add_fusion
  3.2 0.4 select_reduce_fusion
  3.6 0.6 broadcast_add_fusion
  4.2 4.8 %copy.28.refs_0_.refs_1_ = bf16[32,128,300]{2,1,0:T(8,128)(2,1)} copy(bf16[32,128,300]{1,0,2:T(8,128)(2,1)} %param.10) | data formatting | bytes 4915200 | tf_op args[2]
  9.0 20.0 %shard_map.82 = bf16[64,304,128]{2,1,0:T(8,128)(2,1)} custom-call(s32[64]{0:T(128)} %select_reduce_fusion.1.source_ref, bf16[32,128,300]{2,1,0:T(8,128)(2,1)} %copy.28.refs_0_.refs_1_, bf16[32,128,300]{2,1,0:T(8,128)(2,1)} %copy.28.refs_0_.refs_1_, s32[32,2,128]{2,1,0:T(2,128)} %bitcast.71), custom_call_target="tpu_custom_call" | custom-call | tf_op jit(solution)/shard_map/pallas_call | solution.py:99
  29.0 7.7 %all-to-all-start = ((bf16[64,304,128]{2,1,0:T(8,128)(2,1)}), bf16[64,304,128]{2,1,0:T(8,128)(2,1)}, u32[]{:S(2)}, u32[]{:S(2)}) async-start(bf16[64,304,128]{2,1,0:T(8,128)(2,1)} %shard_map.82), calls=%async_computation | async-start | bytes 9961472 | tf_op jit(solution)/shard_map/all_to_all | solution.py:164
  36.7 1.3 fusion.14
  38.0 1.7 collective-permute-start.5
  39.7 2.1 collective-permute-start.4
  41.8 1.3 fusion.15
  43.2 1.8 collective-permute-start
  44.9 0.3 collective-permute-start.1
  45.3 93.1 %collective-permute-done.5 = f32[360,4,128]{2,1,0:T(4,128)} collective-permute-done((f32[360,4,128]{2,1,0:T(4,128)}, f32[360,4,128]{2,1,0:T(4,128)}, u32[]{:S(2)}, u32[]{:S(2)}) %collective-permute-start.5) | collective-permute-done | bytes 737312 | tf_op jit(solution)/shard_map/ppermute | solution.py:19
  138.4 0.2 broadcast_select_fusion
  138.6 12.3 %collective-permute-done.4 = f32[360,4,128]{2,1,0:T(4,128)} collective-permute-done((f32[360,4,128]{2,1,0:T(4,128)}, f32[360,4,128]{2,1,0:T(4,128)}, u32[]{:S(2)}, u32[]{:S(2)}) %collective-permute-start.4) | collective-permute-done | bytes 737312 | tf_op jit(solution)/shard_map/ppermute | solution.py:20
  150.9 1.3 broadcast_select_fusion.1
  152.2 0.4 pad_maximum_fusion.2.coef_ref
  152.6 3.5 fusion.11
  156.1 3.1 copy.34
  159.2 1.7 collective-permute-start.6
  160.9 3.1 copy.35
  164.1 3.3 collective-permute-done
  167.4 18.0 %collective-permute-done.1 = f32[360,4,128]{2,1,0:T(4,128)} collective-permute-done((f32[360,4,128]{2,1,0:T(4,128)}, f32[360,4,128]{2,1,0:T(4,128)}, u32[]{:S(2)}, u32[]{:S(2)}) %collective-permute-start.1) | collective-permute-done | bytes 737312 | tf_op jit(solution)/shard_map/ppermute | solution.py:19
  185.4 1.7 pad_maximum_fusion.field_ref
  187.1 2.6 fusion.12
  189.7 3.1 copy.30
  192.8 0.7 reshape.85
  193.5 2.2 collective-permute-start.2
  195.7 1.5 copy.31
  197.2 0.7 reshape.86
  197.9 1.0 pad_maximum_fusion.7
  198.9 1.7 copy.47
  200.7 3.1 copy.48
  203.8 1.6 pad_maximum_fusion.6
  205.4 1.0 reshape.87
  206.4 0.7 fusion.19
  207.0 4.1 copy.45
  211.1 3.2 copy.46
  214.3 8.0 %pad_maximum_fusion.3 = (f32[360,16,128]{2,1,0:T(8,128)}, f32[360,16,128]{2,1,0:T(8,128)}) fusion(f32[360,16,4]{2,1,0:T(8,128)} %bitcast.59, f32[360,16,4]{2,1,0:T(8,128)S(1)} %bitcast.58, f32[128]{0:T(128)S(1)} %pad.17.clone, f32[360,16,4]{2,1,0:T(8,128)} %bitcast.61, f32[360,16,4]{2,1,0:T(8,128)} %bitcast.60), kind=kLoop, calls=%fused_computation.3 | loop fusion | flops 2949120 | bytes 6267392 | tf_op jit(solution)/shard_map/concatenate | solution.py:39
  222.3 54.1 %shard_map.84 = f32[360,8,128]{2,1,0:T(8,128)} custom-call(f32[360,16,128]{2,1,0:T(8,128)} %copy-done.2, f32[360,16,128]{2,1,0:T(8,128)} %get-tuple-element.24.side_ref, f32[360,16,128]{2,1,0:T(8,128)} %copy-done.1, f32[360,16,128]{2,1,0:T(8,128)} %get-tuple-element.23.coef_side_ref), custom_call_target="tpu_custom_call" | custom-call | flops 58982400 | bytes 14745600 | tf_op jit(solution)/shard_map/pallas_call | solution.py:66
  276.3 1.4 convert_element_type.10
  277.8 13.2 %shard_map.83 = f32[304,1024]{1,0:T(8,128)S(1)} custom-call(bf16[64,304,128]{2,1,0:T(8,128)(2,1)} %all-to-all-done.refs_0_), custom_call_target="tpu_custom_call" | custom-call | tf_op jit(solution)/shard_map/pallas_call | solution.py:137
  291.0 0.5 fusion.3
  291.5 0.4 copy.44
  291.9 0.1 fusion.16
  292.1 25.5 %collective-permute-start.9 = (bf16[300,4,128]{0,2,1:T(8,128)(2,1)S(1)}, bf16[300,4,128]{0,2,1:T(8,128)(2,1)S(1)}, u32[]{:S(2)}, u32[]{:S(2)}) collective-permute-start(bf16[300,4,128]{0,2,1:T(8,128)(2,1)S(1)} %get-tuple-element.16), channel_id=1, source_target_pairs={{0,8},{8,16},{16,24},{24,0},{1,9},{9,17},{17,25},{25,1},{2,10},{10... | collective-permute-start | bytes 921608 | tf_op jit(solution)/shard_map/ppermute | solution.py:19
  317.6 9.3 %collective-permute-done.8 = bf16[300,4,128]{0,2,1:T(8,128)(2,1)S(1)} collective-permute-done((bf16[300,4,128]{0,2,1:T(8,128)(2,1)S(1)}, bf16[300,4,128]{0,2,1:T(8,128)(2,1)S(1)}, u32[]{:S(2)}, u32[]{:S(2)}) %collective-permute-start.8) | collective-permute-done | bytes 307232 | tf_op jit(solution)/shard_map/ppermute | solution.py:20
  326.9 9.5 %collective-permute-done.9 = bf16[300,4,128]{0,2,1:T(8,128)(2,1)S(1)} collective-permute-done((bf16[300,4,128]{0,2,1:T(8,128)(2,1)S(1)}, bf16[300,4,128]{0,2,1:T(8,128)(2,1)S(1)}, u32[]{:S(2)}, u32[]{:S(2)}) %collective-permute-start.9) | collective-permute-done | bytes 307232 | tf_op jit(solution)/shard_map/ppermute | solution.py:19
  336.5 0.3 pad_maximum_fusion.5
  336.9 1.9 collective-permute-start.10
  338.8 0.3 collective-permute-start.11
  339.0 1.0 convolution_bitcast_fusion
  340.0 2.2 copy.52
  342.2 1.2 collective-permute-done.11
  343.4 0.3 convolution_bitcast_fusion.1
  343.8 0.1 copy.41
  344.0 1.7 copy.49
  345.7 3.1 copy.50
  348.8 4.4 %pad_maximum_fusion.4.side_ref = f32[360,16,128]{2,1,0:T(8,128)} fusion(f32[360,16,4]{2,1,0:T(8,128)} %bitcast.64, f32[360,16,4]{2,1,0:T(8,128)S(1)} %bitcast.63, f32[128]{0:T(128)S(1)} %pad.17.clone), kind=kLoop, calls=%fused_computation.4 | loop fusion | flops 1474560 | bytes 3133952 | tf_op jit(solution)/shard_map/concatenate | solution.py:39
  353.2 54.2 %shard_map.85 = f32[360,8,128]{2,1,0:T(8,128)} custom-call(f32[360,16,128]{2,1,0:T(8,128)} %bitcast.62, f32[360,16,128]{2,1,0:T(8,128)} %pad_maximum_fusion.4.side_ref, f32[360,16,128]{2,1,0:T(8,128)} %copy-done.1, f32[360,16,128]{2,1,0:T(8,128)} %get-tuple-element.23.coef_side_ref, f32[360,8,128]{2,1,0:T(8,128)} %bitcast.55), custom_call_target="tpu_custom_call" | custom-call | flops 58982400 | bytes 14745600 | tf_op jit(solution)/shard_map/pallas_call | solution.py:66
  (34 shorter events, 0.7 us)
Async XLA Ops:
  0.0 291.0 %copy-start = (bf16[360,300]{0,1:T(8,128)(2,1)S(1)}, bf16[360,300]{0,1:T(8,128)(2,1)}, u32[]{:S(2)}) copy-start(bf16[360,300]{0,1:T(8,128)(2,1)} %param.14) | copy-start | bytes 648004
  29.0 7.7 %copy-start.4 = (f32[4,90,8,128]{3,2,1,0:T(8,128)S(1)}, f32[4,90,8,128]{3,2,1,0:T(8,128)}, u32[]{:S(2)}) copy-start(f32[4,90,8,128]{3,2,1,0:T(8,128)} %param.9) | copy-start | bytes 4423684
  29.0 248.8 %all-to-all-start = ((bf16[64,304,128]{2,1,0:T(8,128)(2,1)}), bf16[64,304,128]{2,1,0:T(8,128)(2,1)}, u32[]{:S(2)}, u32[]{:S(2)}) async-start(bf16[64,304,128]{2,1,0:T(8,128)(2,1)} %shard_map.82), calls=%async_computation | async-start | bytes 9961472 | tf_op jit(solution)/shard_map/all_to_all | solution.py:164
  36.6 5.2 %copy-start.3 = (f32[4,90,8,128]{3,2,1,0:T(8,128)S(1)}, f32[4,90,8,128]{3,2,1,0:T(8,128)}, u32[]{:S(2)}) copy-start(f32[4,90,8,128]{3,2,1,0:T(8,128)} %param.8) | copy-start | bytes 4423684
  38.0 100.4 %collective-permute-start.5 = (f32[360,4,128]{2,1,0:T(4,128)}, f32[360,4,128]{2,1,0:T(4,128)}, u32[]{:S(2)}, u32[]{:S(2)}) collective-permute-start(f32[360,4,128]{2,1,0:T(4,128)} %get-tuple-element.12), channel_id=1, source_target_pairs={{0,8},{8,16},{16,24},{24,0},{1,9},{9,17},{17,25},{25,1},{2,10},{10... | collective-permute-start | bytes 2211848 | tf_op jit(solution)/shard_map/ppermute | solution.py:19
  39.7 111.2 %collective-permute-start.4 = (f32[360,4,128]{2,1,0:T(4,128)}, f32[360,4,128]{2,1,0:T(4,128)}, u32[]{:S(2)}, u32[]{:S(2)}) collective-permute-start(f32[360,4,128]{2,1,0:T(4,128)} %get-tuple-element.11), channel_id=1, source_target_pairs={{0,24},{8,0},{16,8},{24,16},{1,25},{9,1},{17,9},{25,17},{2,26},{10... | collective-permute-start | bytes 2211848 | tf_op jit(solution)/shard_map/ppermute | solution.py:20
  43.2 124.2 %collective-permute-start = (f32[360,4,128]{2,1,0:T(4,128)}, f32[360,4,128]{2,1,0:T(4,128)}, u32[]{:S(2)}, u32[]{:S(2)}) collective-permute-start(f32[360,4,128]{2,1,0:T(4,128)} %get-tuple-element.13), channel_id=1, source_target_pairs={{0,24},{8,0},{16,8},{24,16},{1,25},{9,1},{17,9},{25,17},{2,26},{10... | collective-permute-start | bytes 2211848 | tf_op jit(solution)/shard_map/ppermute | solution.py:20
  44.9 140.4 %collective-permute-start.1 = (f32[360,4,128]{2,1,0:T(4,128)}, f32[360,4,128]{2,1,0:T(4,128)}, u32[]{:S(2)}, u32[]{:S(2)}) collective-permute-start(f32[360,4,128]{2,1,0:T(4,128)} %get-tuple-element.14), channel_id=1, source_target_pairs={{0,8},{8,16},{16,24},{24,0},{1,9},{9,17},{17,25},{25,1},{2,10},{10... | collective-permute-start | bytes 2211848 | tf_op jit(solution)/shard_map/ppermute | solution.py:19
  152.6 3.5 copy-start.1
  159.2 38.7 %collective-permute-start.6 = (f32[360,64]{0,1:T(8,128)S(1)}, f32[360,64]{0,1:T(8,128)}, u32[]{:S(2)}, u32[]{:S(2)}) collective-permute-start(f32[360,64]{0,1:T(8,128)S(1)} %reshape.89), channel_id=1, source_target_pairs={{0,7},{1,0},{2,1},{3,2},{4,3},{5,4},{6,5},{7,6},{8,15},{9,8},{10,9... | collective-permute-start | bytes 276488 | tf_op jit(solution)/shard_map/ppermute | solution.py:31
  164.1 33.8 %collective-permute-start.7 = (f32[360,64]{0,1:T(8,128)S(1)}, f32[360,64]{0,1:T(8,128)}, u32[]{:S(2)}, u32[]{:S(2)}) collective-permute-start(f32[360,64]{0,1:T(8,128)S(1)} %reshape.90), channel_id=1, source_target_pairs={{0,1},{1,2},{2,3},{3,4},{4,5},{5,6},{6,7},{7,0},{8,9},{9,10},{10,1... | collective-permute-start | bytes 276488 | tf_op jit(solution)/shard_map/ppermute | solution.py:30
  187.1 2.6 copy-start.2
  193.5 10.3 %collective-permute-start.2 = (f32[360,64]{0,1:T(8,128)}, f32[360,64]{0,1:T(8,128)}, u32[]{:S(2)}, u32[]{:S(2)}) collective-permute-start(f32[360,64]{0,1:T(8,128)} %reshape.85), channel_id=1, source_target_pairs={{0,7},{1,0},{2,1},{3,2},{4,3},{5,4},{6,5},{7,6},{8,15},{9,8},{10,9... | collective-permute-start | bytes 276488 | tf_op jit(solution)/shard_map/ppermute | solution.py:31
  197.9 5.9 %collective-permute-start.3 = (f32[360,64]{0,1:T(8,128)}, f32[360,64]{0,1:T(8,128)}, u32[]{:S(2)}, u32[]{:S(2)}) collective-permute-start(f32[360,64]{0,1:T(8,128)} %reshape.86), channel_id=1, source_target_pairs={{0,1},{1,2},{2,3},{3,4},{4,5},{5,6},{6,7},{7,0},{8,9},{9,10},{10,1... | collective-permute-start | bytes 276488 | tf_op jit(solution)/shard_map/ppermute | solution.py:30
  277.8 13.2 %copy-start.5 = (f32[300]{0:T(512)S(1)}, f32[300]{0:T(512)}, u32[]{:S(2)}) copy-start(f32[300]{0:T(512)} %param.15) | copy-start | bytes 3604
  292.0 34.9 %collective-permute-start.8 = (bf16[300,4,128]{0,2,1:T(8,128)(2,1)S(1)}, bf16[300,4,128]{0,2,1:T(8,128)(2,1)S(1)}, u32[]{:S(2)}, u32[]{:S(2)}) collective-permute-start(bf16[300,4,128]{0,2,1:T(8,128)(2,1)S(1)} %get-tuple-element.15), channel_id=1, source_target_pairs={{0,24},{8,0},{16,8},{24,16},{1,25},{9,1},{17,9},{25,17},{2,26},{10... | collective-permute-start | bytes 921608 | tf_op jit(solution)/shard_map/ppermute | solution.py:20
  292.1 44.4 %collective-permute-start.9 = (bf16[300,4,128]{0,2,1:T(8,128)(2,1)S(1)}, bf16[300,4,128]{0,2,1:T(8,128)(2,1)S(1)}, u32[]{:S(2)}, u32[]{:S(2)}) collective-permute-start(bf16[300,4,128]{0,2,1:T(8,128)(2,1)S(1)} %get-tuple-element.16), channel_id=1, source_target_pairs={{0,8},{8,16},{16,24},{24,0},{1,9},{9,17},{17,25},{25,1},{2,10},{10... | collective-permute-start | bytes 921608 | tf_op jit(solution)/shard_map/ppermute | solution.py:19
  336.9 5.3 %collective-permute-start.10 = (bf16[300,64]{0,1:T(8,128)(2,1)S(1)}, bf16[300,64]{0,1:T(8,128)(2,1)S(1)}, u32[]{:S(2)}, u32[]{:S(2)}) collective-permute-start(bf16[300,64]{0,1:T(8,128)(2,1)S(1)} %reshape.96), channel_id=1, source_target_pairs={{0,7},{1,0},{2,1},{3,2},{4,3},{5,4},{6,5},{7,6},{8,15},{9,8},{10,9... | collective-permute-start | bytes 115208 | tf_op jit(solution)/shard_map/ppermute | solution.py:31
  338.8 4.7 %collective-permute-start.11 = (bf16[300,64]{0,1:T(8,128)(2,1)S(1)}, bf16[300,64]{0,1:T(8,128)(2,1)S(1)}, u32[]{:S(2)}, u32[]{:S(2)}) collective-permute-start(bf16[300,64]{0,1:T(8,128)(2,1)S(1)} %reshape.97), channel_id=1, source_target_pairs={{0,1},{1,2},{2,3},{3,4},{4,5},{5,6},{6,7},{7,0},{8,9},{9,10},{10,1... | collective-permute-start | bytes 115208 | tf_op jit(solution)/shard_map/ppermute | solution.py:30
where the time goes:
time: 409 us; the launch traced here: 407 us
  waiting for transfers between devices  147 us (36%)
  Pallas kernels  141 us (34%)
  local copies, waits for them, and re-layouts  47.5 us (12%)
  starting transfers between devices  45.2 us (11%)
  other arithmetic  24.4 us (6%)
    ppermute x3, waiting for transfers between devices, rims(): north = lax.ppermute(core[:, -STEPS:], 'lat', ring('lat', 1))  121 us
    pallas_call x2, Pallas kernels, spread(): pl.pallas_call(spread_kernel, out_shape=jax.ShapeDtypeStruct((planes, cor...  108 us
    ppermute x3, starting transfers between devices, rims(): north = lax.ppermute(core[:, -STEPS:], 'lat', ring('lat', 1))  27.5 us
    ppermute x3, waiting for transfers between devices, rims(): south = lax.ppermute(core[:, :STEPS], 'lat', ring('lat', -1))  25 us
    unnamed x20, local copies, waits for them, and re-layouts  23.8 us
    pallas_call x1, Pallas kernels, pack(): pl.pallas_call(pack_kernel, out_shape=jax.ShapeDtypeStruct((slots, height...  20 us
    pallas_call x1, Pallas kernels, column_sums(): pl.pallas_call(lambda *refs: gather_kernel(comps, *refs), out_shape=jax.S...  13.2 us
    concatenate x2, other arithmetic, side_tile(): return jnp.concatenate([parts[:, 0], gap, parts[:, 1]], axis=2)  12.4 us
  transfers between devices with their start and end apart: 13, of which 7 were waited for; matrix products, arithmetic and copies ran while one was open for 13% of the time, Pallas kernels for 13%

commit v1 on v0

--- a/solution.py
+++ b/solution.py
@@ -161,13 +161,13 @@
     code = jnp.where(order[None, :] < counts[:, None], columns, -32)
     code = -32 + jnp.sum(jnp.where(hits[:, :, None], code[None] + 32, 0), axis=1)
     sent = pack(pc_obs, source, code, height)
-    got = lax.all_to_all(sent, ("lat", "lon"), split_axis=0, concat_axis=0, tiled=True)
-
     planes = fields * levels
     extent = rows + 2 * STEPS
     start = control.reshape(planes, rows, width_dev)
     field, side = rims(start, False)
     coef, coef_side = rims(kappa.reshape(planes, rows, width_dev), True)
+    sent, side, coef_side = lax.optimization_barrier((sent, side, coef_side))
+    got = lax.all_to_all(sent, ("lat", "lon"), split_axis=0, concat_axis=0, tiled=True)
     coef_side = side_tile(coef_side, extent, width_dev)
     state = spread(field, side_tile(side, extent, width_dev), coef, coef_side, rows)
     table = state.astype(jnp.bfloat16).reshape(planes, cells)

time: 409 us -> 309 us (0.76)
  waiting for transfers between devices: 147 us -> 70.1 us
  starting transfers between devices: 45.2 us -> 26.5 us
    ppermute x3, waiting for transfers between devices: 121 us -> 14 us  [rims(): north = lax.ppermute(core[:, -STEPS:], 'lat', ring('lat', 1))]
    all_to_all x1, waiting for transfers between devices: 0.01 us -> 32.8 us  [per_device(): lax.all_to_all(sent, ('lat', 'lon'), split_axis=0, concat_axis=0, tiled=T...]
    ppermute x3, starting transfers between devices: 27.5 us -> 3.09 us  [rims(): north = lax.ppermute(core[:, -STEPS:], 'lat', ring('lat', 1))]
    ppermute x3, starting transfers between devices: 3.96 us -> 9.66 us  [rims(): south = lax.ppermute(core[:, :STEPS], 'lat', ring('lat', -1))]
    unnamed x20 -> x30, local copies, waits for them, and re-layouts: 23.8 us -> 22.4 us
  transfers between devices with their start and end apart: 13 -> 13, of which waited for: 7 -> 7; matrix products, arithmetic and copies ran while one was open for 13% -> 17% of each run, Pallas kernels for 13% -> 24%
where the time goes in v1:
time: 309 us; the launch traced here: 308 us
  Pallas kernels  142 us (46%)
  waiting for transfers between devices  70.1 us (23%)
  local copies, waits for them, and re-layouts  45.7 us (15%)
  starting transfers between devices  26.5 us (9%)
  other arithmetic  21.5 us (7%)
    pallas_call x2, Pallas kernels, spread(): pl.pallas_call(spread_kernel, out_shape=jax.ShapeDtypeStruct((planes, cor...  108 us
    all_to_all x1, waiting for transfers between devices, per_device(): lax.all_to_all(sent, ('lat', 'lon'), split_axis=0, concat_axis=0, tiled=T...  32.8 us
    unnamed x30, local copies, waits for them, and re-layouts  22.4 us
    ppermute x3, waiting for transfers between devices, rims(): south = lax.ppermute(core[:, :STEPS], 'lat', ring('lat', -1))  22 us
    pallas_call x1, Pallas kernels, pack(): pl.pallas_call(pack_kernel, out_shape=jax.ShapeDtypeStruct((slots, height...  20.4 us
    ppermute x3, waiting for transfers between devices, rims(): north = lax.ppermute(core[:, -STEPS:], 'lat', ring('lat', 1))  14 us
    pallas_call x1, Pallas kernels, column_sums(): pl.pallas_call(lambda *refs: gather_kernel(comps, *refs), out_shape=jax.S...  13.2 us
    concatenate x2, other arithmetic, side_tile(): return jnp.concatenate([parts[:, 0], gap, parts[:, 1]], axis=2)  12.4 us
  transfers between devices with their start and end apart: 13, of which 7 were waited for; matrix products, arithmetic and copies ran while one was open for 17% of the time, Pallas kernels for 24%

profile of v1, /device:TPU:0, one launch (start us, length us, event | category | flops | bytes accessed | tf_op | source)
XLA Modules:
  0.0 307.8 jit_solution(15343900207680689625)
XLA Ops:
  0.0 3.3 %fusion.15 = (f32[360,4,128]{2,1,0:T(4,128)}, f32[360,4,128]{2,1,0:T(4,128)}) fusion(f32[360,8,128]{2,1,0:T(8,128)} %bitcast.55), kind=kLoop, calls=%fused_computation.37 | loop fusion | bytes 2949120 | tf_op jit(solution)/shard_map/slice | solution.py:20
  3.4 3.0 collective-permute-start.1
  6.4 2.0 collective-permute-start
  8.4 1.4 fusion.14
  9.8 3.8 %collective-permute-start.4 = (f32[360,4,128]{2,1,0:T(4,128)}, f32[360,4,128]{2,1,0:T(4,128)}, u32[]{:S(2)}, u32[]{:S(2)}) collective-permute-start(f32[360,4,128]{2,1,0:T(4,128)} %get-tuple-element.17), channel_id=1, source_target_pairs={{0,24},{8,0},{16,8},{24,16},{1,25},{9,1},{17,9},{25,17},{2,26},{10... | collective-permute-start | bytes 2211848 | tf_op jit(solution)/shard_map/ppermute | solution.py:20
  13.7 0.2 convert_reduce_fusion
  13.9 0.1 iota_compare_fusion.1
  13.9 3.3 %copy.28.refs_0_.refs_1_ = bf16[32,128,300]{2,1,0:T(8,128)(2,1)} copy(bf16[32,128,300]{1,0,2:T(8,128)(2,1)S(1)} %copy-done.6) | data formatting | bytes 4915200 | tf_op args[2]
  17.2 0.1 copy.27
  17.4 0.1 select_add_fusion
  17.4 0.4 select_reduce_fusion
  17.8 0.6 broadcast_add_fusion
  18.4 0.7 select_reduce_fusion.1.source_ref
  19.1 20.4 %shard_map.82 = bf16[64,304,128]{2,1,0:T(8,128)(2,1)} custom-call(s32[64]{0:T(128)} %select_reduce_fusion.1.source_ref, bf16[32,128,300]{2,1,0:T(8,128)(2,1)} %copy.28.refs_0_.refs_1_, bf16[32,128,300]{2,1,0:T(8,128)(2,1)} %copy.28.refs_0_.refs_1_, s32[32,2,128]{2,1,0:T(2,128)} %bitcast.71), custom_call_target="tpu_custom_call" | custom-call | tf_op jit(solution)/shard_map/pallas_call | solution.py:99
  39.5 2.5 collective-permute-done
  42.1 1.6 pad_maximum_fusion.field_ref
  43.7 2.6 fusion.12
  46.2 3.1 %copy.31 = f32[360,16,4]{0,2,1:T(4,128)S(1)} copy(f32[360,16,4]{2,1,0:T(8,128)} %get-tuple-element.14) | data formatting | bytes 184320 | tf_op jit(solution)/shard_map/slice | solution.py:29
  49.4 1.5 copy.30
  51.0 2.7 collective-permute-start.2
  53.7 4.0 %collective-permute-done.5 = f32[360,4,128]{2,1,0:T(4,128)} collective-permute-done((f32[360,4,128]{2,1,0:T(4,128)}, f32[360,4,128]{2,1,0:T(4,128)}, u32[]{:S(2)}, u32[]{:S(2)}) %collective-permute-start.5) | collective-permute-done | bytes 737312 | tf_op jit(solution)/shard_map/ppermute | solution.py:19
  57.7 0.2 broadcast_select_fusion
  57.9 14.2 %collective-permute-done.4 = f32[360,4,128]{2,1,0:T(4,128)} collective-permute-done((f32[360,4,128]{2,1,0:T(4,128)}, f32[360,4,128]{2,1,0:T(4,128)}, u32[]{:S(2)}, u32[]{:S(2)}) %collective-permute-start.4) | collective-permute-done | bytes 737312 | tf_op jit(solution)/shard_map/ppermute | solution.py:20
  72.1 1.3 broadcast_select_fusion.1
  73.3 0.4 pad_maximum_fusion.1.coef_ref
  73.8 2.6 fusion.11
  76.3 3.1 %copy.33 = f32[360,16,4]{0,2,1:T(4,128)S(1)} copy(f32[360,16,4]{2,1,0:T(8,128)} %get-tuple-element.12) | data formatting | bytes 184320 | tf_op jit(solution)/shard_map/slice | solution.py:29
  79.4 0.7 reshape.89
  80.1 1.5 copy.32
  81.7 2.7 collective-permute-start.6
  84.4 1.0 pad_maximum_fusion.6
  85.4 1.2 collective-permute-done.6
  86.6 0.9 pad_maximum_fusion.7
  87.5 5.4 %all-to-all-start = ((bf16[64,304,128]{2,1,0:T(8,128)(2,1)}), bf16[64,304,128]{2,1,0:T(8,128)(2,1)}, u32[]{:S(2)}, u32[]{:S(2)}) async-start(bf16[64,304,128]{2,1,0:T(8,128)(2,1)} %shard_map.82), calls=%async_computation | async-start | bytes 9961472 | tf_op jit(solution)/shard_map/all_to_all | solution.py:170
  92.9 0.1 pad.12.clone
  93.0 0.7 fusion.18
  93.7 2.6 copy.48
  96.3 3.1 copy.47
  99.4 0.7 reshape.90
  100.1 1.0 fusion.19
  101.1 3.2 %copy.46 = f32[360,1,16,4]{3,2,0,1:T(8,128)} copy(f32[360,1,16,4]{0,3,2,1:T(4,128)S(1)} %get-tuple-element.28) | data formatting | bytes 184320
  104.3 3.2 %copy.45 = f32[360,1,16,4]{3,2,0,1:T(8,128)} copy(f32[360,1,16,4]{0,3,2,1:T(4,128)S(1)} %get-tuple-element.27) | data formatting | bytes 184320
  107.4 8.0 %pad_maximum_fusion.3 = (f32[360,16,128]{2,1,0:T(8,128)}, f32[360,16,128]{2,1,0:T(8,128)}) fusion(f32[360,16,4]{2,1,0:T(8,128)S(1)} %bitcast.58, f32[360,16,4]{2,1,0:T(8,128)} %bitcast.59, f32[128]{0:T(128)S(1)} %pad.12.clone, f32[360,16,4]{2,1,0:T(8,128)} %bitcast.60, f32[360,16,4]{2,1,0:T(8,128)} %bitcast.61), kind=kLoop, calls=%fused_computation.3 | loop fusion | flops 2949120 | bytes 6267392 | tf_op jit(solution)/shard_map/concatenate | solution.py:39
  115.4 54.1 %shard_map.84 = f32[360,8,128]{2,1,0:T(8,128)} custom-call(f32[360,16,128]{2,1,0:T(8,128)} %copy-done.2, f32[360,16,128]{2,1,0:T(8,128)} %get-tuple-element.30.side_ref, f32[360,16,128]{2,1,0:T(8,128)} %copy-done.1, f32[360,16,128]{2,1,0:T(8,128)} %get-tuple-element.29.coef_side_ref), custom_call_target="tpu_custom_call" | custom-call | flops 58982400 | bytes 14745600 | tf_op jit(solution)/shard_map/pallas_call | solution.py:66
  169.5 1.4 convert_element_type.10
  171.0 32.8 %all-to-all-done.refs_0_ = bf16[64,304,128]{2,1,0:T(8,128)(2,1)} async-done(((bf16[64,304,128]{2,1,0:T(8,128)(2,1)}), bf16[64,304,128]{2,1,0:T(8,128)(2,1)}, u32[]{:S(2)}, u32[]{:S(2)}) %all-to-all-start) | async-done | bytes 4980768 | tf_op jit(solution)/shard_map/all_to_all | solution.py:170
  203.8 13.2 %shard_map.83 = f32[304,1024]{1,0:T(8,128)S(1)} custom-call(bf16[64,304,128]{2,1,0:T(8,128)(2,1)} %all-to-all-done.refs_0_), custom_call_target="tpu_custom_call" | custom-call | tf_op jit(solution)/shard_map/pallas_call | solution.py:137
  217.0 0.5 fusion.3
  217.5 0.4 copy.44
  217.9 0.1 fusion.16
  218.0 3.8 %collective-permute-start.8 = (bf16[300,4,128]{0,2,1:T(8,128)(2,1)S(1)}, bf16[300,4,128]{0,2,1:T(8,128)(2,1)S(1)}, u32[]{:S(2)}, u32[]{:S(2)}) collective-permute-start(bf16[300,4,128]{0,2,1:T(8,128)(2,1)S(1)} %get-tuple-element.21), channel_id=1, source_target_pairs={{0,24},{8,0},{16,8},{24,16},{1,25},{9,1},{17,9},{25,17},{2,26},{10... | collective-permute-start | bytes 921608 | tf_op jit(solution)/shard_map/ppermute | solution.py:20
  221.9 10.0 %collective-permute-done.9 = bf16[300,4,128]{0,2,1:T(8,128)(2,1)S(1)} collective-permute-done((bf16[300,4,128]{0,2,1:T(8,128)(2,1)S(1)}, bf16[300,4,128]{0,2,1:T(8,128)(2,1)S(1)}, u32[]{:S(2)}, u32[]{:S(2)}) %collective-permute-start.9) | collective-permute-done | bytes 307232 | tf_op jit(solution)/shard_map/ppermute | solution.py:19
  231.9 5.3 %collective-permute-done.8 = bf16[300,4,128]{0,2,1:T(8,128)(2,1)S(1)} collective-permute-done((bf16[300,4,128]{0,2,1:T(8,128)(2,1)S(1)}, bf16[300,4,128]{0,2,1:T(8,128)(2,1)S(1)}, u32[]{:S(2)}, u32[]{:S(2)}) %collective-permute-start.8) | collective-permute-done | bytes 307232 | tf_op jit(solution)/shard_map/ppermute | solution.py:20
  237.2 0.3 pad_maximum_fusion.5
  237.7 2.9 collective-permute-start.10
  240.6 1.0 convolution_bitcast_fusion
  241.6 2.2 copy.52
  243.8 0.3 convolution_bitcast_fusion.1
  244.1 0.1 copy.41
  244.2 0.1 reshape.98
  244.3 1.7 copy.50
  246.0 3.1 %copy.49 = f32[360,1,16,4]{3,2,0,1:T(8,128)} copy(f32[360,1,16,4]{0,3,2,1:T(4,128)S(1)} %get-tuple-element.23) | data formatting | bytes 184320
  249.2 4.4 %pad_maximum_fusion.4.side_ref = f32[360,16,128]{2,1,0:T(8,128)} fusion(f32[360,16,4]{2,1,0:T(8,128)S(1)} %bitcast.63, f32[360,16,4]{2,1,0:T(8,128)} %bitcast.64, f32[128]{0:T(128)S(1)} %pad.12.clone), kind=kLoop, calls=%fused_computation.4 | loop fusion | flops 1474560 | bytes 3133952 | tf_op jit(solution)/shard_map/concatenate | solution.py:39
  253.6 54.2 %shard_map.85 = f32[360,8,128]{2,1,0:T(8,128)} custom-call(f32[360,16,128]{2,1,0:T(8,128)} %bitcast.62, f32[360,16,128]{2,1,0:T(8,128)} %pad_maximum_fusion.4.side_ref, f32[360,16,128]{2,1,0:T(8,128)} %copy-done.1, f32[360,16,128]{2,1,0:T(8,128)} %get-tuple-element.29.coef_side_ref, f32[360,8,128]{2,1,0:T(8,128)} %bitcast.56), custom_call_target="tpu_custom_call" | custom-call | flops 58982400 | bytes 14745600 | tf_op jit(solution)/shard_map/pallas_call | solution.py:66
  (44 shorter events, 0.6 us)
Async XLA Ops:
  0.0 217.0 %copy-start = (bf16[360,300]{0,1:T(8,128)(2,1)S(1)}, bf16[360,300]{0,1:T(8,128)(2,1)}, u32[]{:S(2)}) copy-start(bf16[360,300]{0,1:T(8,128)(2,1)} %param.14) | copy-start | bytes 648004
  0.0 8.4 %copy-start.4 = (f32[4,90,8,128]{3,2,1,0:T(8,128)S(1)}, f32[4,90,8,128]{3,2,1,0:T(8,128)}, u32[]{:S(2)}) copy-start(f32[4,90,8,128]{3,2,1,0:T(8,128)} %param.9) | copy-start | bytes 4423684
  0.0 13.7 %copy-start.10 = (s32[32,1]{0,1:T(1,128)S(1)}, s32[32,1]{0,1:T(1,128)}, u32[]{:S(2)}) copy-start(s32[32,1]{0,1:T(1,128)} %param.11) | copy-start | bytes 388
  0.0 13.9 %copy-start.6 = (bf16[32,128,300]{1,0,2:T(8,128)(2,1)S(1)}, bf16[32,128,300]{1,0,2:T(8,128)(2,1)}, u32[]{:S(2)}) copy-start(bf16[32,128,300]{1,0,2:T(8,128)(2,1)} %param.10) | copy-start | bytes 7372804
  3.4 36.2 %collective-permute-start.1 = (f32[360,4,128]{2,1,0:T(4,128)}, f32[360,4,128]{2,1,0:T(4,128)S(1)}, u32[]{:S(2)}, u32[]{:S(2)}) collective-permute-start(f32[360,4,128]{2,1,0:T(4,128)} %get-tuple-element.20), channel_id=1, source_target_pairs={{0,8},{8,16},{16,24},{24,0},{1,9},{9,17},{17,25},{25,1},{2,10},{10... | collective-permute-start | bytes 2211848 | tf_op jit(solution)/shard_map/ppermute | solution.py:19
  6.4 35.7 %collective-permute-start = (f32[360,4,128]{2,1,0:T(4,128)}, f32[360,4,128]{2,1,0:T(4,128)}, u32[]{:S(2)}, u32[]{:S(2)}) collective-permute-start(f32[360,4,128]{2,1,0:T(4,128)} %get-tuple-element.19), channel_id=1, source_target_pairs={{0,24},{8,0},{16,8},{24,16},{1,25},{9,1},{17,9},{25,17},{2,26},{10... | collective-permute-start | bytes 2211848 | tf_op jit(solution)/shard_map/ppermute | solution.py:20
  9.8 7.5 %copy-start.7 = (s32[32,128]{1,0:T(8,128)S(1)}, s32[32,128]{1,0:T(8,128)}, u32[]{:S(2)}) copy-start(s32[32,128]{1,0:T(8,128)} %param.12) | copy-start | bytes 49156
  9.8 7.5 %copy-start.8 = (s32[32]{0:T(128)S(1)}, s32[32]{0:T(128)}, u32[]{:S(2)}) copy-start(s32[32]{0:T(128)} %param.13) | copy-start | bytes 388
  9.8 47.9 %collective-permute-start.5 = (f32[360,4,128]{2,1,0:T(4,128)}, f32[360,4,128]{2,1,0:T(4,128)}, u32[]{:S(2)}, u32[]{:S(2)}) collective-permute-start(f32[360,4,128]{2,1,0:T(4,128)} %get-tuple-element.18), channel_id=1, source_target_pairs={{0,8},{8,16},{16,24},{24,0},{1,9},{9,17},{17,25},{25,1},{2,10},{10... | collective-permute-start | bytes 2211848 | tf_op jit(solution)/shard_map/ppermute | solution.py:19
  9.8 62.2 %collective-permute-start.4 = (f32[360,4,128]{2,1,0:T(4,128)}, f32[360,4,128]{2,1,0:T(4,128)}, u32[]{:S(2)}, u32[]{:S(2)}) collective-permute-start(f32[360,4,128]{2,1,0:T(4,128)} %get-tuple-element.17), channel_id=1, source_target_pairs={{0,24},{8,0},{16,8},{24,16},{1,25},{9,1},{17,9},{25,17},{2,26},{10... | collective-permute-start | bytes 2211848 | tf_op jit(solution)/shard_map/ppermute | solution.py:20
  19.1 23.0 %copy-start.3 = (f32[4,90,8,128]{3,2,1,0:T(8,128)S(1)}, f32[4,90,8,128]{3,2,1,0:T(8,128)}, u32[]{:S(2)}) copy-start(f32[4,90,8,128]{3,2,1,0:T(8,128)} %param.8) | copy-start | bytes 4423684
  43.7 2.6 copy-start.2
  49.4 35.0 %collective-permute-start.3 = (f32[360,64]{0,1:T(8,128)S(1)}, f32[360,64]{0,1:T(8,128)}, u32[]{:S(2)}, u32[]{:S(2)}) collective-permute-start(f32[360,64]{0,1:T(8,128)S(1)} %reshape.86), channel_id=1, source_target_pairs={{0,1},{1,2},{2,3},{3,4},{4,5},{5,6},{6,7},{7,0},{8,9},{9,10},{10,1... | collective-permute-start | bytes 276488 | tf_op jit(solution)/shard_map/ppermute | solution.py:30
  51.0 22.4 %copy-start.5 = (f32[4,90,8,128]{3,2,1,0:T(8,128)S(1)}, f32[4,90,8,128]{3,2,1,0:T(8,128)}, u32[]{:S(2)}) copy-start(f32[4,90,8,128]{3,2,1,0:T(8,128)} %param.9) | copy-start | bytes 4423684
  51.0 33.4 %collective-permute-start.2 = (f32[360,64]{0,1:T(8,128)S(1)}, f32[360,64]{0,1:T(8,128)}, u32[]{:S(2)}, u32[]{:S(2)}) collective-permute-start(f32[360,64]{0,1:T(8,128)S(1)} %reshape.85), channel_id=1, source_target_pairs={{0,7},{1,0},{2,1},{3,2},{4,3},{5,4},{6,5},{7,6},{8,15},{9,8},{10,9... | collective-permute-start | bytes 276488 | tf_op jit(solution)/shard_map/ppermute | solution.py:31
  73.7 2.6 copy-start.1
  80.1 5.3 %collective-permute-start.7 = (f32[360,64]{0,1:T(8,128)}, f32[360,64]{0,1:T(8,128)}, u32[]{:S(2)}, u32[]{:S(2)}) collective-permute-start(f32[360,64]{0,1:T(8,128)} %reshape.89), channel_id=1, source_target_pairs={{0,1},{1,2},{2,3},{3,4},{4,5},{5,6},{6,7},{7,0},{8,9},{9,10},{10,1... | collective-permute-start | bytes 276488 | tf_op jit(solution)/shard_map/ppermute | solution.py:30
  81.7 4.9 %collective-permute-start.6 = (f32[360,64]{0,1:T(8,128)S(1)}, f32[360,64]{0,1:T(8,128)S(1)}, u32[]{:S(2)}, u32[]{:S(2)}) collective-permute-start(f32[360,64]{0,1:T(8,128)S(1)} %reshape.88), channel_id=1, source_target_pairs={{0,7},{1,0},{2,1},{3,2},{4,3},{5,4},{6,5},{7,6},{8,15},{9,8},{10,9... | collective-permute-start | bytes 276488 | tf_op jit(solution)/shard_map/ppermute | solution.py:31
  87.5 116.3 %all-to-all-start = ((bf16[64,304,128]{2,1,0:T(8,128)(2,1)}), bf16[64,304,128]{2,1,0:T(8,128)(2,1)}, u32[]{:S(2)}, u32[]{:S(2)}) async-start(bf16[64,304,128]{2,1,0:T(8,128)(2,1)} %shard_map.82), calls=%async_computation | async-start | bytes 9961472 | tf_op jit(solution)/shard_map/all_to_all | solution.py:170
  170.9 46.1 %copy-start.9 = (f32[300]{0:T(512)S(1)}, f32[300]{0:T(512)}, u32[]{:S(2)}) copy-start(f32[300]{0:T(512)} %param.15) | copy-start | bytes 3604
  218.0 13.9 %collective-permute-start.9 = (bf16[300,4,128]{0,2,1:T(8,128)(2,1)S(1)}, bf16[300,4,128]{0,2,1:T(8,128)(2,1)S(1)}, u32[]{:S(2)}, u32[]{:S(2)}) collective-permute-start(bf16[300,4,128]{0,2,1:T(8,128)(2,1)S(1)} %get-tuple-element.22), channel_id=1, source_target_pairs={{0,8},{8,16},{16,24},{24,0},{1,9},{9,17},{17,25},{25,1},{2,10},{10... | collective-permute-start | bytes 921608 | tf_op jit(solution)/shard_map/ppermute | solution.py:19
  218.0 19.1 %collective-permute-start.8 = (bf16[300,4,128]{0,2,1:T(8,128)(2,1)S(1)}, bf16[300,4,128]{0,2,1:T(8,128)(2,1)S(1)}, u32[]{:S(2)}, u32[]{:S(2)}) collective-permute-start(bf16[300,4,128]{0,2,1:T(8,128)(2,1)S(1)} %get-tuple-element.21), channel_id=1, source_target_pairs={{0,24},{8,0},{16,8},{24,16},{1,25},{9,1},{17,9},{25,17},{2,26},{10... | collective-permute-start | bytes 921608 | tf_op jit(solution)/shard_map/ppermute | solution.py:20
  237.6 6.2 %collective-permute-start.11 = (bf16[300,64]{0,1:T(8,128)(2,1)S(1)}, bf16[300,64]{0,1:T(8,128)(2,1)S(1)}, u32[]{:S(2)}, u32[]{:S(2)}) collective-permute-start(bf16[300,64]{0,1:T(8,128)(2,1)S(1)} %reshape.97), channel_id=1, source_target_pairs={{0,1},{1,2},{2,3},{3,4},{4,5},{5,6},{6,7},{7,0},{8,9},{9,10},{10,1... | collective-permute-start | bytes 115208 | tf_op jit(solution)/shard_map/ppermute | solution.py:30
  237.7 6.1 %collective-permute-start.10 = (bf16[300,64]{0,1:T(8,128)(2,1)S(1)}, bf16[300,64]{0,1:T(8,128)(2,1)S(1)}, u32[]{:S(2)}, u32[]{:S(2)}) collective-permute-start(bf16[300,64]{0,1:T(8,128)(2,1)S(1)} %reshape.96), channel_id=1, source_target_pairs={{0,7},{1,0},{2,1},{3,2},{4,3},{5,4},{6,5},{7,6},{8,15},{9,8},{10,9... | collective-permute-start | bytes 115208 | tf_op jit(solution)/shard_map/ppermute | solution.py:31

commit v2 on v1

--- a/solution.py
+++ b/solution.py
@@ -32,47 +32,65 @@
     return main, jnp.concatenate([east, west], axis=1)
 
 
-def side_tile(side, rows, width):
-    planes = side.shape[0]
-    parts = side.reshape(planes, 2, rows, STEPS)
-    gap = jnp.zeros((planes, rows, width - 2 * STEPS), side.dtype)
-    return jnp.concatenate([parts[:, 0], gap, parts[:, 1]], axis=2)
-
-
-def spread_kernel(field_ref, side_ref, coef_ref, coef_side_ref, *refs):
+def strips(main, side, fields):
+    planes, rows, width = main.shape
+    levels, near = planes // fields, 3 * STEPS
+    body = main.reshape(fields, levels, rows, width)
+    flat = side.reshape(fields, levels, 2, rows, STEPS)
+    pieces = []
+    for f in range(fields):
+        pieces += [flat[f, :, 1], body[f, :, :, :near], body[f, :, :, width - near :], flat[f, :, 0]]
+    return jnp.concatenate(pieces, axis=2)
+
+
+def diffused(field, coef):
+    rows, lanes = field.shape
+    south = coef * pltpu.roll(coef, rows - 1, 0)
+    east = coef * pltpu.roll(coef, lanes - 1, 1)
+    for repeat in range(STEPS):
+        down = south * (pltpu.roll(field, rows - 1, 0) - field)
+        along = east * (pltpu.roll(field, lanes - 1, 1) - field)
+        field = field + (down - pltpu.roll(down, 1, 0)) + (along - pltpu.roll(along, 1, 1))
+    return field
+
+
+def spread_kernel(field_ref, strip_ref, coef_ref, coef_strip_ref, *refs):
     out_ref = refs[-1]
-    core, width = out_ref.shape[1:]
-    rows, lanes = field_ref.shape[1], 2 * width
-
-    @pl.loop(0, out_ref.shape[0], unroll=4)
+    fields, levels, core, width = out_ref.shape
+    slot = 8 * STEPS
+    lane = lax.broadcasted_iota(jnp.int32, (core, width), 1)
+
+    @pl.loop(0, levels)
     def _(i):
-        coef = jnp.concatenate([coef_ref[i], coef_side_ref[i]], axis=1)
-        field = jnp.concatenate([field_ref[i], side_ref[i]], axis=1)
-        south = coef * pltpu.roll(coef, rows - 1, 0)
-        east = coef * pltpu.roll(coef, lanes - 1, 1)
-        for repeat in range(STEPS):
-            down = south * (pltpu.roll(field, rows - 1, 0) - field)
-            along = east * (pltpu.roll(field, lanes - 1, 1) - field)
-            field = field + (down - pltpu.roll(down, 1, 0)) + (along - pltpu.roll(along, 1, 1))
-        result = field[:core, :width]
-        out_ref[i] = result + refs[0][i] if len(refs) > 1 else result
-
-
-def spread(field, side, coef, coef_side, core, *base):
+        edge = diffused(strip_ref[i], coef_strip_ref[i])[:core]
+        for f in range(fields):
+            result = diffused(field_ref[f, i], coef_ref[f, i])[:core]
+            west = pltpu.roll(edge, (width - slot * f - STEPS) % width, 1)
+            east = pltpu.roll(edge, (width - slot * f - slot + STEPS) % width, 1)
+            result = jnp.where(lane < STEPS, west, result)
+            result = jnp.where(lane >= width - STEPS, east, result)
+            out_ref[f, i] = result + refs[0][f, i] if len(refs) > 1 else result
+
+
+def spread(field, strip, coef, coef_strip, core, *base):
     planes, rows, width = field.shape
-    batch = max(n for n in range(4, 41, 4) if planes % n == 0)
-    wide = pl.BlockSpec((batch, rows, width), lambda i: (i, 0, 0))
-    thin = pl.BlockSpec((batch, core, width), lambda i: (i, 0, 0))
+    levels = strip.shape[0]
+    fields = planes // levels
+    batch = max(n for n in range(1, 11) if levels % n == 0)
+    wide = pl.BlockSpec((fields, batch, rows, width), lambda i: (0, i, 0, 0))
+    edge = pl.BlockSpec((batch, rows, strip.shape[2]), lambda i: (i, 0, 0))
+    thin = pl.BlockSpec((fields, batch, core, width), lambda i: (0, i, 0, 0))
+    shape = (fields, levels, rows, width)
     return pl.pallas_call(
         spread_kernel,
-        out_shape=jax.ShapeDtypeStruct((planes, core, width), jnp.float32),
-        grid=(planes // batch,),
-        in_specs=[wide] * 4 + [thin] * len(base),
+        out_shape=jax.ShapeDtypeStruct((fields, levels, core, width), jnp.float32),
+        grid=(levels // batch,),
+        in_specs=[wide, edge, wide, edge] + [thin] * len(base),
         out_specs=thin,
         cost_estimate=pl.CostEstimate(
-            flops=planes * rows * width * 80, bytes_accessed=planes * rows * width * 20, transcendentals=0
+            flops=planes * rows * width * 50, bytes_accessed=planes * rows * width * 14, transcendentals=0
         ),
-    )(field, side, coef, coef_side, *base)
+    )(field.reshape(shape), strip, coef.reshape(shape), coef_strip, *base)
 
 
 def pack_kernel(source_ref, *refs):
@@ -168,8 +186,8 @@
     coef, coef_side = rims(kappa.reshape(planes, rows, width_dev), True)
     sent, side, coef_side = lax.optimization_barrier((sent, side, coef_side))
     got = lax.all_to_all(sent, ("lat", "lon"), split_axis=0, concat_axis=0, tiled=True)
-    coef_side = side_tile(coef_side, extent, width_dev)
-    state = spread(field, side_tile(side, extent, width_dev), coef, coef_side, rows)
+    coef_side = strips(coef, coef_side, fields)
+    state = spread(field, strips(field, side, fields), coef, coef_side, rows)
     table = state.astype(jnp.bfloat16).reshape(planes, cells)
     model = lax.dot_general(
         jacobian, table, (((0,), (0,)), ((), ())), preferred_element_type=jnp.float32
@@ -185,8 +203,7 @@
         for part in (total, total_side)
     )
     back = back.reshape(planes, extent, width_dev)
-    result = spread(back, side_tile(back_side, extent, width_dev), coef, coef_side, rows, start)
-    return result.reshape(control.shape)
+    return spread(back, strips(back, back_side, fields), coef, coef_side, rows, control)
 
 
 def solution(mesh):

time: 309 us -> 337 us (1.091)
  local copies, waits for them, and re-layouts: 45.7 us -> 111 us
  waiting for transfers between devices: 70.1 us -> 30 us
  Pallas kernels: 142 us -> 152 us
  other arithmetic: 21.5 us -> 12.9 us
    all_to_all x1, waiting for transfers between devices: 32.8 us -> 0.01 us  [per_device(): lax.all_to_all(sent, ('lat', 'lon'), split_axis=0, concat_axis=0, tiled=T...]
    concatenate x1 -> x3, local copies, waits for them, and re-layouts: 0.07 us -> 22.5 us  [strips(): return jnp.concatenate(pieces, axis=2)]
    unnamed x30 -> x66, local copies, waits for them, and re-layouts: 22.4 us -> 43.8 us
    concatenate x2 -> x0, other arithmetic: 12.4 us -> none  [side_tile(): return jnp.concatenate([parts[:, 0], gap, parts[:, 1]], axis=2)]
    pallas_call x2, Pallas kernels: 108 us -> 118 us  [spread(): pl.pallas_call(spread_kernel, out_shape=jax.ShapeDtypeStruct((fields, lev...]
    squeeze x0 -> x3, local copies, waits for them, and re-layouts: none -> 9.46 us  [strips(): body[f, :, :, width - near:]]
    slice x5, local copies, waits for them, and re-layouts: 8.23 us -> 13.2 us  [rims(): head = main[:, :, :STEPS].reshape(planes, -1)]
    ppermute x3, waiting for transfers between devices: 14 us -> 10 us  [rims(): north = lax.ppermute(core[:, -STEPS:], 'lat', ring('lat', 1))]
  transfers between devices with their start and end apart: 13 -> 13, of which waited for: 7 -> 4; matrix products, arithmetic and copies ran while one was open for 17% -> 29% of each run, Pallas kernels for 24% -> 24%
where the time goes in v2:
time: 337 us; the launch traced here: 334 us
  Pallas kernels  152 us (45%)
  local copies, waits for them, and re-layouts  111 us (33%)
  waiting for transfers between devices  30 us (9%)
  starting transfers between devices  27 us (8%)
  other arithmetic  12.9 us (4%)
    pallas_call x2, Pallas kernels, spread(): pl.pallas_call(spread_kernel, out_shape=jax.ShapeDtypeStruct((fields, lev...  118 us
    unnamed x66, local copies, waits for them, and re-layouts  43.8 us
    concatenate x3, local copies, waits for them, and re-layouts, strips(): return jnp.concatenate(pieces, axis=2)  22.5 us
    pallas_call x1, Pallas kernels, pack(): pl.pallas_call(pack_kernel, out_shape=jax.ShapeDtypeStruct((slots, height...  20.3 us
    ppermute x3, waiting for transfers between devices, rims(): south = lax.ppermute(core[:, :STEPS], 'lat', ring('lat', -1))  19.1 us
    slice x5, local copies, waits for them, and re-layouts, rims(): head = main[:, :, :STEPS].reshape(planes, -1)  13.2 us
    pallas_call x1, Pallas kernels, column_sums(): pl.pallas_call(lambda *refs: gather_kernel(comps, *refs), out_shape=jax.S...  13.2 us
    ppermute x3, waiting for transfers between devices, rims(): north = lax.ppermute(core[:, -STEPS:], 'lat', ring('lat', 1))  10 us
  transfers between devices with their start and end apart: 13, of which 4 were waited for; matrix products, arithmetic and copies ran while one was open for 29% of the time, Pallas kernels for 24%

profile of v2, /device:TPU:0, one launch (start us, length us, event | category | flops | bytes accessed | tf_op | source)
XLA Modules:
  0.0 334.5 jit_solution(3742104407000455789)
XLA Ops:
  0.0 2.2 fusion.15
  3.1 3.0 collective-permute-start.1
  7.1 2.0 collective-permute-start
  11.2 3.8 %collective-permute-start.4 = (f32[360,4,128]{2,0,1:T(8,128)}, f32[360,4,128]{2,0,1:T(8,128)}, u32[]{:S(2)}, u32[]{:S(2)}) collective-permute-start(f32[360,4,128]{2,0,1:T(8,128)} %copy.144), channel_id=1, source_target_pairs={{0,24},{8,0},{16,8},{24,16},{1,25},{9,1},{17,9},{25,17},{2,26},{10... | collective-permute-start | bytes 2211848 | tf_op jit(solution)/shard_map/ppermute | solution.py:20
  15.3 4.8 %copy.136.refs_0_.refs_1_ = bf16[32,128,300]{2,1,0:T(8,128)(2,1)} copy(bf16[32,128,300]{1,0,2:T(8,128)(2,1)} %param.10) | data formatting | bytes 4915200 | tf_op args[2]
  21.8 20.3 %shard_map.82 = bf16[64,304,128]{2,1,0:T(8,128)(2,1)} custom-call(s32[64]{0:T(128)} %select_reduce_fusion.1.source_ref, bf16[32,128,300]{2,1,0:T(8,128)(2,1)} %copy.136.refs_0_.refs_1_, bf16[32,128,300]{2,1,0:T(8,128)(2,1)} %copy.136.refs_0_.refs_1_, s32[32,2,128]{2,1,0:T(2,128)} %bitcast.164), custom_call_target="tpu_custom_call" | custom-call | tf_op jit(solution)/shard_map/pallas_call | solution.py:117
  42.1 1.4 copy.141
  43.6 1.6 copy.140
  46.4 3.5 %fusion.12 = (f32[360,16,4]{2,1,0:T(8,128)}, f32[360,16,4]{2,1,0:T(8,128)}) fusion(f32[360,16,128]{2,1,0:T(8,128)S(1)} %pad_maximum_fusion), kind=kLoop, calls=%fused_computation.57 | loop fusion | bytes 368640 | tf_op jit(solution)/shard_map/slice | solution.py:28
  49.9 3.1 copy.143
  53.1 3.1 copy.142
  56.3 2.7 collective-permute-start.2
  58.9 1.3 copy_select_fusion
  60.3 12.1 %collective-permute-done.4 = f32[360,4,128]{2,0,1:T(8,128)} collective-permute-done((f32[360,4,128]{2,0,1:T(8,128)}, f32[360,4,128]{2,0,1:T(8,128)}, u32[]{:S(2)}, u32[]{:S(2)}) %collective-permute-start.4) | collective-permute-done | bytes 737312 | tf_op jit(solution)/shard_map/ppermute | solution.py:20
  72.4 1.3 copy_select_fusion.1
  75.0 3.5 %fusion.11 = (f32[360,16,4]{2,1,0:T(8,128)}, f32[360,16,4]{2,1,0:T(8,128)}) fusion(f32[360,16,128]{2,1,0:T(8,128)S(1)} %pad_maximum_fusion.1), kind=kLoop, calls=%fused_computation.56 | loop fusion | bytes 368640 | tf_op jit(solution)/shard_map/slice | solution.py:28
  78.4 3.1 copy.149
  82.2 3.1 copy.148
  86.0 2.6 collective-permute-start.6
  88.7 1.6 pad_maximum_fusion.5
  91.2 1.6 pad_maximum_fusion.6
  92.8 6.1 %all-to-all-start = ((bf16[64,304,128]{2,1,0:T(8,128)(2,1)}), bf16[64,304,128]{2,1,0:T(8,128)(2,1)}, u32[]{:S(2)}, u32[]{:S(2)}) async-start(bf16[64,304,128]{2,1,0:T(8,128)(2,1)} %shard_map.82), calls=%async_computation | async-start | bytes 9961472 | tf_op jit(solution)/shard_map/all_to_all | solution.py:188
  98.9 2.6 pad_maximum_fusion.2
  101.5 3.7 %slice_bitcast_fusion.16 = (f32[90,16,12]{2,1,0:T(8,128)}, f32[90,16,12]{2,1,0:T(8,128)}, f32[90,16,12]{2,1,0:T(8,128)}, f32[90,16,12]{2,1,0:T(8,128)}, f32[90,1...) fusion(f32[4,90,16,128]{3,2,1,0:T(8,128)S(1)} %get-tuple-element.71.field_ref), kind=kLoop, calls=%fused_computation.31 | loop fusion | bytes 1105920 | tf_op jit(solution)/shard_map/squeeze | solution.py:42
  105.9 2.4 slice_bitcast_fusion.8
  108.3 1.1 reshape.97
  110.3 2.0 copy.181
  112.3 2.0 copy.182
  114.3 2.0 copy.183
  116.3 2.0 copy.184
  118.3 1.2 copy.185
  119.5 1.2 copy.186
  120.8 1.2 copy.187
  122.0 1.3 copy.188
  123.3 1.1 reshape.98
  125.2 2.0 copy.189
  127.3 2.0 copy.190
  129.3 2.0 copy.191
  131.3 2.0 copy.192
  133.3 1.3 copy.193
  134.5 1.3 copy.194
  135.8 1.3 copy.195
  137.1 1.2 copy.196
  138.3 7.8 %concatenate.48.strip_ref = f32[90,16,128]{2,1,0:T(8,128)} concatenate(f32[90,16,4]{2,1,0:T(8,128)} %bitcast.139, f32[90,16,12]{2,1,0:T(8,128)} %get-tuple-element.34, f32[90,16,12]{2,1,0:T(8,128)} %get-tuple-element.33, f32[90,16,4]{2,1,0:T(8,128)} %bitcast.140, f32[90,16,4]{2,1,0:T(8,128)} %bitcast.141, f32[90,16,12]{2,1,0:T(8,128)} %get-tuple-element.32, ...), dimensions={2} | concatenate | bytes 1474560 | tf_op jit(solution)/shard_map/concatenate | solution.py:43
  146.1 7.3 %concatenate.52.coef_strip_ref = f32[90,16,128]{2,1,0:T(8,128)} concatenate(f32[90,16,4]{2,1,0:T(8,128)} %bitcast.147, f32[90,16,12]{2,1,0:T(8,128)} %get-tuple-element.26, f32[90,16,12]{2,1,0:T(8,128)} %get-tuple-element.25, f32[90,16,4]{2,1,0:T(8,128)} %bitcast.148, f32[90,16,4]{2,1,0:T(8,128)} %bitcast.149, f32[90,16,12]{2,1,0:T(8,128)} %get-tuple-element.24, ...), dimensions={2} | concatenate | bytes 1474560 | tf_op jit(solution)/shard_map/concatenate | solution.py:43
  153.5 59.0 %shard_map.84 = f32[4,90,8,128]{3,2,1,0:T(8,128)} custom-call(f32[4,90,16,128]{3,2,1,0:T(8,128)} %copy-done.2, f32[90,16,128]{2,1,0:T(8,128)} %concatenate.48.strip_ref, f32[4,90,16,128]{3,2,1,0:T(8,128)} %copy-done.1, f32[90,16,128]{2,1,0:T(8,128)} %concatenate.52.coef_strip_ref), custom_call_target="tpu_custom_call" | custom-call | flops 36864000 | bytes 10321920 | tf_op jit(solution)/shard_map/pallas_call | solution.py:84
  212.5 1.5 convert_element_type.10
  214.0 13.2 %shard_map.83 = f32[304,1024]{1,0:T(8,128)S(1)} custom-call(bf16[64,304,128]{2,1,0:T(8,128)(2,1)} %all-to-all-done.refs_0_), custom_call_target="tpu_custom_call" | custom-call | tf_op jit(solution)/shard_map/pallas_call | solution.py:155
  228.2 1.6 collective-permute-start.9
  229.8 2.3 collective-permute-start.8
  232.1 10.0 %collective-permute-done.9 = bf16[300,4,128]{0,2,1:T(8,128)(2,1)S(1)} collective-permute-done((bf16[300,4,128]{0,2,1:T(8,128)(2,1)S(1)}, bf16[300,4,128]{0,2,1:T(8,128)(2,1)S(1)}, u32[]{:S(2)}, u32[]{:S(2)}) %collective-permute-start.9) | collective-permute-done | bytes 307232 | tf_op jit(solution)/shard_map/ppermute | solution.py:19
  242.1 7.0 %collective-permute-done.8 = bf16[300,4,128]{0,2,1:T(8,128)(2,1)S(1)} collective-permute-done((bf16[300,4,128]{0,2,1:T(8,128)(2,1)S(1)}, bf16[300,4,128]{0,2,1:T(8,128)(2,1)S(1)}, u32[]{:S(2)}, u32[]{:S(2)}) %collective-permute-start.8) | collective-permute-done | bytes 307232 | tf_op jit(solution)/shard_map/ppermute | solution.py:20
  251.2 2.7 collective-permute-start.10
  253.9 3.3 slice_bitcast_fusion
  258.0 1.2 copy.197
  259.3 1.2 copy.198
  260.5 1.2 copy.199
  261.8 1.3 copy.200
  263.0 1.2 copy.201
  264.2 1.2 copy.202
  265.5 1.2 copy.203
  266.7 1.2 copy.204
  268.0 7.3 %concatenate.55.strip_ref = f32[90,16,128]{2,1,0:T(8,128)} concatenate(f32[90,16,4]{2,1,0:T(8,128)} %bitcast.155, f32[90,16,12]{2,1,0:T(8,128)} %get-tuple-element.18, f32[90,16,12]{2,1,0:T(8,128)} %get-tuple-element.17, f32[90,16,4]{2,1,0:T(8,128)} %bitcast.156, f32[90,16,4]{2,1,0:T(8,128)} %bitcast.157, f32[90,16,12]{2,1,0:T(8,128)} %get-tuple-element.16, ...), dimensions={2} | concatenate | bytes 1474560 | tf_op jit(solution)/shard_map/concatenate | solution.py:43
  275.3 59.2 %shard_map.85 = f32[4,90,8,128]{3,2,1,0:T(8,128)} custom-call(f32[4,90,16,128]{3,2,1,0:T(8,128)} %bitcast.127, f32[90,16,128]{2,1,0:T(8,128)} %concatenate.55.strip_ref, f32[4,90,16,128]{3,2,1,0:T(8,128)} %copy-done.1, f32[90,16,128]{2,1,0:T(8,128)} %concatenate.52.coef_strip_ref, f32[4,90,8,128]{3,2,1,0:T(8,128)} %refs_0_.2), custom_call_target="tpu_custom_call" | custom-call | flops 36864000 | bytes 10321920 | tf_op jit(solution)/shard_map/pallas_call | solution.py:84
  (89 shorter events, 17.0 us)
Async XLA Ops:
  0.0 227.2 %copy-start = (bf16[360,300]{0,1:T(8,128)(2,1)S(1)}, bf16[360,300]{0,1:T(8,128)(2,1)}, u32[]{:S(2)}) copy-start(bf16[360,300]{0,1:T(8,128)(2,1)} %param.14) | copy-start | bytes 648004
  0.0 9.1 %copy-start.5 = (f32[4,90,8,128]{3,2,1,0:T(8,128)S(1)}, f32[4,90,8,128]{3,2,1,0:T(8,128)}, u32[]{:S(2)}) copy-start(f32[4,90,8,128]{3,2,1,0:T(8,128)} %param.9) | copy-start | bytes 4423684
  3.1 39.0 %collective-permute-start.1 = (f32[360,4,128]{2,0,1:T(8,128)}, f32[360,4,128]{2,0,1:T(8,128)}, u32[]{:S(2)}, u32[]{:S(2)}) collective-permute-start(f32[360,4,128]{2,0,1:T(8,128)} %copy.139), channel_id=1, source_target_pairs={{0,8},{8,16},{16,24},{24,0},{1,9},{9,17},{17,25},{25,1},{2,10},{10... | collective-permute-start | bytes 2211848 | tf_op jit(solution)/shard_map/ppermute | solution.py:19
  7.1 36.5 %collective-permute-start = (f32[360,4,128]{2,0,1:T(8,128)}, f32[360,4,128]{2,0,1:T(8,128)}, u32[]{:S(2)}, u32[]{:S(2)}) collective-permute-start(f32[360,4,128]{2,0,1:T(8,128)} %copy.138), channel_id=1, source_target_pairs={{0,24},{8,0},{16,8},{24,16},{1,25},{9,1},{17,9},{25,17},{2,26},{10... | collective-permute-start | bytes 2211848 | tf_op jit(solution)/shard_map/ppermute | solution.py:20
  9.1 5.9 %copy-start.19 = (s32[32,1]{0,1:T(1,128)S(1)}, s32[32,1]{0,1:T(1,128)}, u32[]{:S(2)}) copy-start(s32[32,1]{0,1:T(1,128)} %param.11) | copy-start | bytes 388
  10.3 48.7 %collective-permute-start.5 = (f32[360,4,128]{2,0,1:T(8,128)}, f32[360,4,128]{2,0,1:T(8,128)}, u32[]{:S(2)}, u32[]{:S(2)}) collective-permute-start(f32[360,4,128]{2,0,1:T(8,128)} %copy.146), channel_id=1, source_target_pairs={{0,8},{8,16},{16,24},{24,0},{1,9},{9,17},{17,25},{25,1},{2,10},{10... | collective-permute-start | bytes 2211848 | tf_op jit(solution)/shard_map/ppermute | solution.py:19
  11.2 9.0 %copy-start.16 = (s32[32,128]{1,0:T(8,128)S(1)}, s32[32,128]{1,0:T(8,128)}, u32[]{:S(2)}) copy-start(s32[32,128]{1,0:T(8,128)} %param.12) | copy-start | bytes 49156
  11.2 9.0 %copy-start.17 = (s32[32]{0:T(128)S(1)}, s32[32]{0:T(128)}, u32[]{:S(2)}) copy-start(s32[32]{0:T(128)} %param.13) | copy-start | bytes 388
  11.2 61.2 %collective-permute-start.4 = (f32[360,4,128]{2,0,1:T(8,128)}, f32[360,4,128]{2,0,1:T(8,128)}, u32[]{:S(2)}, u32[]{:S(2)}) collective-permute-start(f32[360,4,128]{2,0,1:T(8,128)} %copy.144), channel_id=1, source_target_pairs={{0,24},{8,0},{16,8},{24,16},{1,25},{9,1},{17,9},{25,17},{2,26},{10... | collective-permute-start | bytes 2211848 | tf_op jit(solution)/shard_map/ppermute | solution.py:20
  42.1 3.9 %copy-start.4 = (f32[4,90,8,128]{3,2,1,0:T(8,128)S(1)}, f32[4,90,8,128]{3,2,1,0:T(8,128)}, u32[]{:S(2)}) copy-start(f32[4,90,8,128]{3,2,1,0:T(8,128)} %refs_0_.2) | copy-start | bytes 4423684
  43.5 1.6 copy-start.6
  45.1 0.9 copy-start.7
  53.0 35.6 %collective-permute-start.3 = (f32[360,64]{0,1:T(8,128)S(1)}, f32[360,64]{0,1:T(8,128)}, u32[]{:S(2)}, u32[]{:S(2)}) collective-permute-start(f32[360,64]{0,1:T(8,128)S(1)} %reshape.93), channel_id=1, source_target_pairs={{0,1},{1,2},{2,3},{3,4},{4,5},{5,6},{6,7},{7,0},{8,9},{9,10},{10,1... | collective-permute-start | bytes 276488 | tf_op jit(solution)/shard_map/ppermute | solution.py:30
  56.3 32.4 %collective-permute-start.2 = (f32[360,64]{0,1:T(8,128)S(1)}, f32[360,64]{0,1:T(8,128)}, u32[]{:S(2)}, u32[]{:S(2)}) collective-permute-start(f32[360,64]{0,1:T(8,128)S(1)} %reshape.92), channel_id=1, source_target_pairs={{0,7},{1,0},{2,1},{3,2},{4,3},{5,4},{6,5},{7,6},{8,15},{9,8},{10,9... | collective-permute-start | bytes 276488 | tf_op jit(solution)/shard_map/ppermute | solution.py:31
  60.2 13.4 %copy-start.8 = (f32[360,4,128]{2,1,0:T(4,128)}, f32[360,4,128]{2,1,0:T(4,128)S(1)}, u32[]{:S(2)}) copy-start(f32[360,4,128]{2,1,0:T(4,128)S(1)} %copy_select_fusion) | copy-start | bytes 2211844
  73.7 0.9 copy-start.9
  82.2 8.1 %collective-permute-start.7 = (f32[360,64]{0,1:T(8,128)}, f32[360,64]{0,1:T(8,128)}, u32[]{:S(2)}, u32[]{:S(2)}) collective-permute-start(f32[360,64]{0,1:T(8,128)} %reshape.96), channel_id=1, source_target_pairs={{0,1},{1,2},{2,3},{3,4},{4,5},{5,6},{6,7},{7,0},{8,9},{9,10},{10,1... | collective-permute-start | bytes 276488 | tf_op jit(solution)/shard_map/ppermute | solution.py:30
  86.0 5.2 %collective-permute-start.6 = (f32[360,64]{0,1:T(8,128)}, f32[360,64]{0,1:T(8,128)S(1)}, u32[]{:S(2)}, u32[]{:S(2)}) collective-permute-start(f32[360,64]{0,1:T(8,128)} %reshape.95), channel_id=1, source_target_pairs={{0,7},{1,0},{2,1},{3,2},{4,3},{5,4},{6,5},{7,6},{8,15},{9,8},{10,9... | collective-permute-start | bytes 276488 | tf_op jit(solution)/shard_map/ppermute | solution.py:31
  92.8 121.2 %all-to-all-start = ((bf16[64,304,128]{2,1,0:T(8,128)(2,1)}), bf16[64,304,128]{2,1,0:T(8,128)(2,1)}, u32[]{:S(2)}, u32[]{:S(2)}) async-start(bf16[64,304,128]{2,1,0:T(8,128)(2,1)} %shard_map.82), calls=%async_computation | async-start | bytes 9961472 | tf_op jit(solution)/shard_map/all_to_all | solution.py:188
  101.5 3.7 %copy-start.2 = (f32[4,90,16,128]{3,2,1,0:T(8,128)}, f32[4,90,16,128]{3,2,1,0:T(8,128)S(1)}, u32[]{:S(2)}) copy-start(f32[4,90,16,128]{3,2,1,0:T(8,128)S(1)} %get-tuple-element.71.field_ref) | copy-start | bytes 8847364
  101.5 4.4 %copy-start.1 = (f32[4,90,16,128]{3,2,1,0:T(8,128)}, f32[4,90,16,128]{3,2,1,0:T(8,128)S(1)}, u32[]{:S(2)}) copy-start(f32[4,90,16,128]{3,2,1,0:T(8,128)S(1)} %get-tuple-element.72.coef_ref) | copy-start | bytes 8847364
  110.3 8.0 %copy-start.14 = (f32[1,90,1,16,4]{1,0,4,3,2:T(1,128)S(1)}, f32[1,90,1,16,4]{1,0,4,3,2:T(1,128)}, u32[]{:S(2)}) copy-start(f32[1,90,1,16,4]{1,0,4,3,2:T(1,128)} %get-tuple-element.66) | copy-start | bytes 69124
  125.2 8.0 %copy-start.15 = (f32[1,90,1,16,4]{1,0,4,3,2:T(1,128)S(1)}, f32[1,90,1,16,4]{1,0,4,3,2:T(1,128)}, u32[]{:S(2)}) copy-start(f32[1,90,1,16,4]{1,0,4,3,2:T(1,128)} %get-tuple-element.58) | copy-start | bytes 69124
  214.0 13.2 %copy-start.18 = (f32[300]{0:T(512)S(1)}, f32[300]{0:T(512)}, u32[]{:S(2)}) copy-start(f32[300]{0:T(512)} %param.15) | copy-start | bytes 3604
  228.2 13.9 %collective-permute-start.9 = (bf16[300,4,128]{0,2,1:T(8,128)(2,1)S(1)}, bf16[300,4,128]{0,2,1:T(8,128)(2,1)S(1)}, u32[]{:S(2)}, u32[]{:S(2)}) collective-permute-start(bf16[300,4,128]{0,2,1:T(8,128)(2,1)S(1)} %get-tuple-element.46), channel_id=1, source_target_pairs={{0,8},{8,16},{16,24},{24,0},{1,9},{9,17},{17,25},{25,1},{2,10},{10... | collective-permute-start | bytes 921608 | tf_op jit(solution)/shard_map/ppermute | solution.py:19
  229.8 19.3 %collective-permute-start.8 = (bf16[300,4,128]{0,2,1:T(8,128)(2,1)S(1)}, bf16[300,4,128]{0,2,1:T(8,128)(2,1)S(1)}, u32[]{:S(2)}, u32[]{:S(2)}) collective-permute-start(bf16[300,4,128]{0,2,1:T(8,128)(2,1)S(1)} %get-tuple-element.45), channel_id=1, source_target_pairs={{0,24},{8,0},{16,8},{24,16},{1,25},{9,1},{17,9},{25,17},{2,26},{10... | collective-permute-start | bytes 921608 | tf_op jit(solution)/shard_map/ppermute | solution.py:20
  251.0 6.1 %copy-start.3 = (f32[45,8,16,128]{3,2,1,0:T(8,128)}, f32[45,8,16,128]{3,2,1,0:T(8,128)S(1)}, u32[]{:S(2)}) copy-start(f32[45,8,16,128]{3,2,1,0:T(8,128)S(1)} %copy.206) | copy-start | bytes 8847364
  251.1 6.1 %collective-permute-start.11 = (bf16[300,64]{0,1:T(8,128)(2,1)S(1)}, bf16[300,64]{0,1:T(8,128)(2,1)S(1)}, u32[]{:S(2)}, u32[]{:S(2)}) collective-permute-start(bf16[300,64]{0,1:T(8,128)(2,1)S(1)} %reshape.103), channel_id=1, source_target_pairs={{0,1},{1,2},{2,3},{3,4},{4,5},{5,6},{6,7},{7,0},{8,9},{9,10},{10,1... | collective-permute-start | bytes 115208 | tf_op jit(solution)/shard_map/ppermute | solution.py:30
  251.2 6.0 %collective-permute-start.10 = (bf16[300,64]{0,1:T(8,128)(2,1)S(1)}, bf16[300,64]{0,1:T(8,128)(2,1)S(1)}, u32[]{:S(2)}, u32[]{:S(2)}) collective-permute-start(bf16[300,64]{0,1:T(8,128)(2,1)S(1)} %reshape.102), channel_id=1, source_target_pairs={{0,7},{1,0},{2,1},{3,2},{4,3},{5,4},{6,5},{7,6},{8,15},{9,8},{10,9... | collective-permute-start | bytes 115208 | tf_op jit(solution)/shard_map/ppermute | solution.py:31
  258.0 10.0 %copy-start.10 = (f32[90,16,12]{2,1,0:T(8,128)S(1)}, f32[90,16,12]{2,1,0:T(8,128)}, u32[]{:S(2)}) copy-start(f32[90,16,12]{2,1,0:T(8,128)} %get-tuple-element.11) | copy-start | bytes 207364
  258.0 10.0 %copy-start.11 = (f32[90,16,12]{2,1,0:T(8,128)S(1)}, f32[90,16,12]{2,1,0:T(8,128)}, u32[]{:S(2)}) copy-start(f32[90,16,12]{2,1,0:T(8,128)} %get-tuple-element.12) | copy-start | bytes 207364
  258.0 10.0 %copy-start.12 = (f32[90,16,12]{2,1,0:T(8,128)S(1)}, f32[90,16,12]{2,1,0:T(8,128)}, u32[]{:S(2)}) copy-start(f32[90,16,12]{2,1,0:T(8,128)} %get-tuple-element.13) | copy-start | bytes 207364
  258.0 9.9 %copy-start.13 = (f32[90,16,12]{2,1,0:T(8,128)S(1)}, f32[90,16,12]{2,1,0:T(8,128)}, u32[]{:S(2)}) copy-start(f32[90,16,12]{2,1,0:T(8,128)} %get-tuple-element.14) | copy-start | bytes 207364

commit v3 on v2

--- a/solution.py
+++ b/solution.py
@@ -43,15 +43,19 @@
     return jnp.concatenate(pieces, axis=2)
 
 
-def diffused(field, coef):
-    rows, lanes = field.shape
-    south = coef * pltpu.roll(coef, rows - 1, 0)
-    east = coef * pltpu.roll(coef, lanes - 1, 1)
+def diffused(tiles, coefs):
+    rows, lanes = tiles[0].shape
+    south = [c * pltpu.roll(c, rows - 1, 0) for c in coefs]
+    east = [c * pltpu.roll(c, lanes - 1, 1) for c in coefs]
     for repeat in range(STEPS):
-        down = south * (pltpu.roll(field, rows - 1, 0) - field)
-        along = east * (pltpu.roll(field, lanes - 1, 1) - field)
-        field = field + (down - pltpu.roll(down, 1, 0)) + (along - pltpu.roll(along, 1, 1))
-    return field
+        below = [pltpu.roll(t, rows - 1, 0) for t in tiles]
+        beside = [pltpu.roll(t, lanes - 1, 1) for t in tiles]
+        down = [w * (n - t) for w, n, t in zip(south, below, tiles)]
+        along = [w * (n - t) for w, n, t in zip(east, beside, tiles)]
+        up = [pltpu.roll(d, 1, 0) for d in down]
+        back = [pltpu.roll(d, 1, 1) for d in along]
+        tiles = [t + (d - u) + (g - h) for t, d, u, g, h in zip(tiles, down, up, along, back)]
+    return tiles
 
 
 def spread_kernel(field_ref, strip_ref, coef_ref, coef_strip_ref, *refs):
@@ -62,14 +66,19 @@
 
     @pl.loop(0, levels)
     def _(i):
-        edge = diffused(strip_ref[i], coef_strip_ref[i])[:core]
+        tiles = [strip_ref[i]] + [field_ref[f, i] for f in range(fields)]
+        coefs = [coef_strip_ref[i]] + [coef_ref[f, i] for f in range(fields)]
+        added = [refs[0][f, i] for f in range(fields)] if len(refs) > 1 else None
+        edge, *results = [t[:core] for t in diffused(tiles, coefs)]
         for f in range(fields):
-            result = diffused(field_ref[f, i], coef_ref[f, i])[:core]
             west = pltpu.roll(edge, (width - slot * f - STEPS) % width, 1)
             east = pltpu.roll(edge, (width - slot * f - slot + STEPS) % width, 1)
-            result = jnp.where(lane < STEPS, west, result)
-            result = jnp.where(lane >= width - STEPS, east, result)
-            out_ref[f, i] = result + refs[0][f, i] if len(refs) > 1 else result
+            results[f] = jnp.where(lane < STEPS, west, results[f])
+            results[f] = jnp.where(lane >= width - STEPS, east, results[f])
+            if added:
+                results[f] = results[f] + added[f]
+        for f in range(fields):
+            out_ref[f, i] = results[f]
 
 
 def spread(field, strip, coef, coef_strip, core, *base):

time: 337 us -> 337 us (level)
  no operation moved by 1% of the time
where the time goes in v3:
time: 337 us; the launch traced here: 334 us
  Pallas kernels  152 us (45%)
  local copies, waits for them, and re-layouts  111 us (33%)
  waiting for transfers between devices  30 us (9%)
  starting transfers between devices  27 us (8%)
  other arithmetic  12.9 us (4%)
    pallas_call x2, Pallas kernels, spread(): pl.pallas_call(spread_kernel, out_shape=jax.ShapeDtypeStruct((fields, lev...  118 us
    unnamed x66, local copies, waits for them, and re-layouts  43.8 us
    concatenate x3, local copies, waits for them, and re-layouts, strips(): return jnp.concatenate(pieces, axis=2)  22.5 us
    pallas_call x1, Pallas kernels, pack(): pl.pallas_call(pack_kernel, out_shape=jax.ShapeDtypeStruct((slots, height...  20.3 us
    ppermute x3, waiting for transfers between devices, rims(): south = lax.ppermute(core[:, :STEPS], 'lat', ring('lat', -1))  19.1 us
    slice x5, local copies, waits for them, and re-layouts, rims(): head = main[:, :, :STEPS].reshape(planes, -1)  13.2 us
    pallas_call x1, Pallas kernels, column_sums(): pl.pallas_call(lambda *refs: gather_kernel(comps, *refs), out_shape=jax.S...  13.2 us
    ppermute x3, waiting for transfers between devices, rims(): north = lax.ppermute(core[:, -STEPS:], 'lat', ring('lat', 1))  10 us
  transfers between devices with their start and end apart: 13, of which 4 were waited for; matrix products, arithmetic and copies ran while one was open for 29% of the time, Pallas kernels for 24%

profile of v3, /device:TPU:0, one launch (start us, length us, event | category | flops | bytes accessed | tf_op | source)
XLA Modules:
  0.0 334.4 jit_solution(1672700784246147451)
XLA Ops:
  0.0 2.2 fusion.15
  3.1 3.0 collective-permute-start.1
  7.1 2.0 collective-permute-start
  11.2 3.8 %collective-permute-start.4 = (f32[360,4,128]{2,0,1:T(8,128)}, f32[360,4,128]{2,0,1:T(8,128)}, u32[]{:S(2)}, u32[]{:S(2)}) collective-permute-start(f32[360,4,128]{2,0,1:T(8,128)} %copy.144), channel_id=1, source_target_pairs={{0,24},{8,0},{16,8},{24,16},{1,25},{9,1},{17,9},{25,17},{2,26},{10... | collective-permute-start | bytes 2211848 | tf_op jit(solution)/shard_map/ppermute | solution.py:20
  15.3 4.8 %copy.136.refs_0_.refs_1_ = bf16[32,128,300]{2,1,0:T(8,128)(2,1)} copy(bf16[32,128,300]{1,0,2:T(8,128)(2,1)} %param.10) | data formatting | bytes 4915200 | tf_op args[2]
  21.8 20.3 %shard_map.82 = bf16[64,304,128]{2,1,0:T(8,128)(2,1)} custom-call(s32[64]{0:T(128)} %select_reduce_fusion.1.source_ref, bf16[32,128,300]{2,1,0:T(8,128)(2,1)} %copy.136.refs_0_.refs_1_, bf16[32,128,300]{2,1,0:T(8,128)(2,1)} %copy.136.refs_0_.refs_1_, s32[32,2,128]{2,1,0:T(2,128)} %bitcast.164), custom_call_target="tpu_custom_call" | custom-call | tf_op jit(solution)/shard_map/pallas_call | solution.py:126
  42.1 1.4 copy.141
  43.5 1.6 copy.140
  46.4 3.5 %fusion.12 = (f32[360,16,4]{2,1,0:T(8,128)}, f32[360,16,4]{2,1,0:T(8,128)}) fusion(f32[360,16,128]{2,1,0:T(8,128)S(1)} %pad_maximum_fusion), kind=kLoop, calls=%fused_computation.57 | loop fusion | bytes 368640 | tf_op jit(solution)/shard_map/slice | solution.py:28
  49.9 3.1 copy.143
  53.1 3.1 copy.142
  56.2 2.7 collective-permute-start.2
  58.9 1.3 copy_select_fusion
  60.3 12.1 %collective-permute-done.4 = f32[360,4,128]{2,0,1:T(8,128)} collective-permute-done((f32[360,4,128]{2,0,1:T(8,128)}, f32[360,4,128]{2,0,1:T(8,128)}, u32[]{:S(2)}, u32[]{:S(2)}) %collective-permute-start.4) | collective-permute-done | bytes 737312 | tf_op jit(solution)/shard_map/ppermute | solution.py:20
  72.4 1.3 copy_select_fusion.1
  75.0 3.5 %fusion.11 = (f32[360,16,4]{2,1,0:T(8,128)}, f32[360,16,4]{2,1,0:T(8,128)}) fusion(f32[360,16,128]{2,1,0:T(8,128)S(1)} %pad_maximum_fusion.1), kind=kLoop, calls=%fused_computation.56 | loop fusion | bytes 368640 | tf_op jit(solution)/shard_map/slice | solution.py:28
  78.4 3.1 copy.149
  82.2 3.1 copy.148
  86.0 2.6 collective-permute-start.6
  88.7 1.6 pad_maximum_fusion.5
  91.2 1.6 pad_maximum_fusion.6
  92.8 6.1 %all-to-all-start = ((bf16[64,304,128]{2,1,0:T(8,128)(2,1)}), bf16[64,304,128]{2,1,0:T(8,128)(2,1)}, u32[]{:S(2)}, u32[]{:S(2)}) async-start(bf16[64,304,128]{2,1,0:T(8,128)(2,1)} %shard_map.82), calls=%async_computation | async-start | bytes 9961472 | tf_op jit(solution)/shard_map/all_to_all | solution.py:197
  98.9 2.6 pad_maximum_fusion.2
  101.5 3.7 %slice_bitcast_fusion.16 = (f32[90,16,12]{2,1,0:T(8,128)}, f32[90,16,12]{2,1,0:T(8,128)}, f32[90,16,12]{2,1,0:T(8,128)}, f32[90,16,12]{2,1,0:T(8,128)}, f32[90,1...) fusion(f32[4,90,16,128]{3,2,1,0:T(8,128)S(1)} %get-tuple-element.71.field_ref), kind=kLoop, calls=%fused_computation.31 | loop fusion | bytes 1105920 | tf_op jit(solution)/shard_map/squeeze | solution.py:42
  105.9 2.4 slice_bitcast_fusion.8
  108.3 1.1 reshape.97
  110.3 2.0 copy.181
  112.3 2.0 copy.182
  114.3 2.0 copy.183
  116.3 2.0 copy.184
  118.3 1.2 copy.185
  119.5 1.2 copy.186
  120.8 1.2 copy.187
  122.0 1.3 copy.188
  123.3 1.1 reshape.98
  125.2 2.0 copy.189
  127.3 2.0 copy.190
  129.3 2.0 copy.191
  131.3 2.0 copy.192
  133.3 1.3 copy.193
  134.5 1.3 copy.194
  135.8 1.3 copy.195
  137.1 1.2 copy.196
  138.3 7.8 %concatenate.48.strip_ref = f32[90,16,128]{2,1,0:T(8,128)} concatenate(f32[90,16,4]{2,1,0:T(8,128)} %bitcast.139, f32[90,16,12]{2,1,0:T(8,128)} %get-tuple-element.34, f32[90,16,12]{2,1,0:T(8,128)} %get-tuple-element.33, f32[90,16,4]{2,1,0:T(8,128)} %bitcast.140, f32[90,16,4]{2,1,0:T(8,128)} %bitcast.141, f32[90,16,12]{2,1,0:T(8,128)} %get-tuple-element.32, ...), dimensions={2} | concatenate | bytes 1474560 | tf_op jit(solution)/shard_map/concatenate | solution.py:43
  146.1 7.3 %concatenate.52.coef_strip_ref = f32[90,16,128]{2,1,0:T(8,128)} concatenate(f32[90,16,4]{2,1,0:T(8,128)} %bitcast.147, f32[90,16,12]{2,1,0:T(8,128)} %get-tuple-element.26, f32[90,16,12]{2,1,0:T(8,128)} %get-tuple-element.25, f32[90,16,4]{2,1,0:T(8,128)} %bitcast.148, f32[90,16,4]{2,1,0:T(8,128)} %bitcast.149, f32[90,16,12]{2,1,0:T(8,128)} %get-tuple-element.24, ...), dimensions={2} | concatenate | bytes 1474560 | tf_op jit(solution)/shard_map/concatenate | solution.py:43
  153.5 59.0 %shard_map.84 = f32[4,90,8,128]{3,2,1,0:T(8,128)} custom-call(f32[4,90,16,128]{3,2,1,0:T(8,128)} %copy-done.2, f32[90,16,128]{2,1,0:T(8,128)} %concatenate.48.strip_ref, f32[4,90,16,128]{3,2,1,0:T(8,128)} %copy-done.1, f32[90,16,128]{2,1,0:T(8,128)} %concatenate.52.coef_strip_ref), custom_call_target="tpu_custom_call" | custom-call | flops 36864000 | bytes 10321920 | tf_op jit(solution)/shard_map/pallas_call | solution.py:93
  212.4 1.5 convert_element_type.10
  213.9 13.2 %shard_map.83 = f32[304,1024]{1,0:T(8,128)S(1)} custom-call(bf16[64,304,128]{2,1,0:T(8,128)(2,1)} %all-to-all-done.refs_0_), custom_call_target="tpu_custom_call" | custom-call | tf_op jit(solution)/shard_map/pallas_call | solution.py:164
  228.1 1.6 collective-permute-start.9
  229.7 2.3 collective-permute-start.8
  232.0 10.0 %collective-permute-done.9 = bf16[300,4,128]{0,2,1:T(8,128)(2,1)S(1)} collective-permute-done((bf16[300,4,128]{0,2,1:T(8,128)(2,1)S(1)}, bf16[300,4,128]{0,2,1:T(8,128)(2,1)S(1)}, u32[]{:S(2)}, u32[]{:S(2)}) %collective-permute-start.9) | collective-permute-done | bytes 307232 | tf_op jit(solution)/shard_map/ppermute | solution.py:19
  242.0 7.0 %collective-permute-done.8 = bf16[300,4,128]{0,2,1:T(8,128)(2,1)S(1)} collective-permute-done((bf16[300,4,128]{0,2,1:T(8,128)(2,1)S(1)}, bf16[300,4,128]{0,2,1:T(8,128)(2,1)S(1)}, u32[]{:S(2)}, u32[]{:S(2)}) %collective-permute-start.8) | collective-permute-done | bytes 307232 | tf_op jit(solution)/shard_map/ppermute | solution.py:20
  251.1 2.7 collective-permute-start.10
  253.8 3.3 slice_bitcast_fusion
  258.0 1.2 copy.197
  259.2 1.2 copy.198
  260.5 1.2 copy.199
  261.7 1.3 copy.200
  263.0 1.2 copy.201
  264.2 1.2 copy.202
  265.4 1.2 copy.203
  266.7 1.2 copy.204
  267.9 7.3 %concatenate.55.strip_ref = f32[90,16,128]{2,1,0:T(8,128)} concatenate(f32[90,16,4]{2,1,0:T(8,128)} %bitcast.155, f32[90,16,12]{2,1,0:T(8,128)} %get-tuple-element.18, f32[90,16,12]{2,1,0:T(8,128)} %get-tuple-element.17, f32[90,16,4]{2,1,0:T(8,128)} %bitcast.156, f32[90,16,4]{2,1,0:T(8,128)} %bitcast.157, f32[90,16,12]{2,1,0:T(8,128)} %get-tuple-element.16, ...), dimensions={2} | concatenate | bytes 1474560 | tf_op jit(solution)/shard_map/concatenate | solution.py:43
  275.3 59.1 %shard_map.85 = f32[4,90,8,128]{3,2,1,0:T(8,128)} custom-call(f32[4,90,16,128]{3,2,1,0:T(8,128)} %bitcast.127, f32[90,16,128]{2,1,0:T(8,128)} %concatenate.55.strip_ref, f32[4,90,16,128]{3,2,1,0:T(8,128)} %copy-done.1, f32[90,16,128]{2,1,0:T(8,128)} %concatenate.52.coef_strip_ref, f32[4,90,8,128]{3,2,1,0:T(8,128)} %refs_0_.2), custom_call_target="tpu_custom_call" | custom-call | flops 36864000 | bytes 10321920 | tf_op jit(solution)/shard_map/pallas_call | solution.py:93
  (89 shorter events, 17.0 us)
Async XLA Ops:
  0.0 227.2 %copy-start = (bf16[360,300]{0,1:T(8,128)(2,1)S(1)}, bf16[360,300]{0,1:T(8,128)(2,1)}, u32[]{:S(2)}) copy-start(bf16[360,300]{0,1:T(8,128)(2,1)} %param.14) | copy-start | bytes 648004
  0.0 9.1 %copy-start.5 = (f32[4,90,8,128]{3,2,1,0:T(8,128)S(1)}, f32[4,90,8,128]{3,2,1,0:T(8,128)}, u32[]{:S(2)}) copy-start(f32[4,90,8,128]{3,2,1,0:T(8,128)} %param.9) | copy-start | bytes 4423684
  3.1 39.0 %collective-permute-start.1 = (f32[360,4,128]{2,0,1:T(8,128)}, f32[360,4,128]{2,0,1:T(8,128)}, u32[]{:S(2)}, u32[]{:S(2)}) collective-permute-start(f32[360,4,128]{2,0,1:T(8,128)} %copy.139), channel_id=1, source_target_pairs={{0,8},{8,16},{16,24},{24,0},{1,9},{9,17},{17,25},{25,1},{2,10},{10... | collective-permute-start | bytes 2211848 | tf_op jit(solution)/shard_map/ppermute | solution.py:19
  7.1 36.5 %collective-permute-start = (f32[360,4,128]{2,0,1:T(8,128)}, f32[360,4,128]{2,0,1:T(8,128)}, u32[]{:S(2)}, u32[]{:S(2)}) collective-permute-start(f32[360,4,128]{2,0,1:T(8,128)} %copy.138), channel_id=1, source_target_pairs={{0,24},{8,0},{16,8},{24,16},{1,25},{9,1},{17,9},{25,17},{2,26},{10... | collective-permute-start | bytes 2211848 | tf_op jit(solution)/shard_map/ppermute | solution.py:20
  9.1 5.9 %copy-start.19 = (s32[32,1]{0,1:T(1,128)S(1)}, s32[32,1]{0,1:T(1,128)}, u32[]{:S(2)}) copy-start(s32[32,1]{0,1:T(1,128)} %param.11) | copy-start | bytes 388
  10.3 48.7 %collective-permute-start.5 = (f32[360,4,128]{2,0,1:T(8,128)}, f32[360,4,128]{2,0,1:T(8,128)}, u32[]{:S(2)}, u32[]{:S(2)}) collective-permute-start(f32[360,4,128]{2,0,1:T(8,128)} %copy.146), channel_id=1, source_target_pairs={{0,8},{8,16},{16,24},{24,0},{1,9},{9,17},{17,25},{25,1},{2,10},{10... | collective-permute-start | bytes 2211848 | tf_op jit(solution)/shard_map/ppermute | solution.py:19
  11.2 9.0 %copy-start.16 = (s32[32,128]{1,0:T(8,128)S(1)}, s32[32,128]{1,0:T(8,128)}, u32[]{:S(2)}) copy-start(s32[32,128]{1,0:T(8,128)} %param.12) | copy-start | bytes 49156
  11.2 9.0 %copy-start.17 = (s32[32]{0:T(128)S(1)}, s32[32]{0:T(128)}, u32[]{:S(2)}) copy-start(s32[32]{0:T(128)} %param.13) | copy-start | bytes 388
  11.2 61.2 %collective-permute-start.4 = (f32[360,4,128]{2,0,1:T(8,128)}, f32[360,4,128]{2,0,1:T(8,128)}, u32[]{:S(2)}, u32[]{:S(2)}) collective-permute-start(f32[360,4,128]{2,0,1:T(8,128)} %copy.144), channel_id=1, source_target_pairs={{0,24},{8,0},{16,8},{24,16},{1,25},{9,1},{17,9},{25,17},{2,26},{10... | collective-permute-start | bytes 2211848 | tf_op jit(solution)/shard_map/ppermute | solution.py:20
  42.1 3.9 %copy-start.4 = (f32[4,90,8,128]{3,2,1,0:T(8,128)S(1)}, f32[4,90,8,128]{3,2,1,0:T(8,128)}, u32[]{:S(2)}) copy-start(f32[4,90,8,128]{3,2,1,0:T(8,128)} %refs_0_.2) | copy-start | bytes 4423684
  43.5 1.6 copy-start.6
  45.1 0.9 copy-start.7
  53.0 35.6 %collective-permute-start.3 = (f32[360,64]{0,1:T(8,128)S(1)}, f32[360,64]{0,1:T(8,128)}, u32[]{:S(2)}, u32[]{:S(2)}) collective-permute-start(f32[360,64]{0,1:T(8,128)S(1)} %reshape.93), channel_id=1, source_target_pairs={{0,1},{1,2},{2,3},{3,4},{4,5},{5,6},{6,7},{7,0},{8,9},{9,10},{10,1... | collective-permute-start | bytes 276488 | tf_op jit(solution)/shard_map/ppermute | solution.py:30
  56.2 32.4 %collective-permute-start.2 = (f32[360,64]{0,1:T(8,128)S(1)}, f32[360,64]{0,1:T(8,128)}, u32[]{:S(2)}, u32[]{:S(2)}) collective-permute-start(f32[360,64]{0,1:T(8,128)S(1)} %reshape.92), channel_id=1, source_target_pairs={{0,7},{1,0},{2,1},{3,2},{4,3},{5,4},{6,5},{7,6},{8,15},{9,8},{10,9... | collective-permute-start | bytes 276488 | tf_op jit(solution)/shard_map/ppermute | solution.py:31
  60.2 13.4 %copy-start.8 = (f32[360,4,128]{2,1,0:T(4,128)}, f32[360,4,128]{2,1,0:T(4,128)S(1)}, u32[]{:S(2)}) copy-start(f32[360,4,128]{2,1,0:T(4,128)S(1)} %copy_select_fusion) | copy-start | bytes 2211844
  73.7 0.9 copy-start.9
  82.2 8.1 %collective-permute-start.7 = (f32[360,64]{0,1:T(8,128)}, f32[360,64]{0,1:T(8,128)}, u32[]{:S(2)}, u32[]{:S(2)}) collective-permute-start(f32[360,64]{0,1:T(8,128)} %reshape.96), channel_id=1, source_target_pairs={{0,1},{1,2},{2,3},{3,4},{4,5},{5,6},{6,7},{7,0},{8,9},{9,10},{10,1... | collective-permute-start | bytes 276488 | tf_op jit(solution)/shard_map/ppermute | solution.py:30
  86.0 5.2 %collective-permute-start.6 = (f32[360,64]{0,1:T(8,128)}, f32[360,64]{0,1:T(8,128)S(1)}, u32[]{:S(2)}, u32[]{:S(2)}) collective-permute-start(f32[360,64]{0,1:T(8,128)} %reshape.95), channel_id=1, source_target_pairs={{0,7},{1,0},{2,1},{3,2},{4,3},{5,4},{6,5},{7,6},{8,15},{9,8},{10,9... | collective-permute-start | bytes 276488 | tf_op jit(solution)/shard_map/ppermute | solution.py:31
  92.8 121.2 %all-to-all-start = ((bf16[64,304,128]{2,1,0:T(8,128)(2,1)}), bf16[64,304,128]{2,1,0:T(8,128)(2,1)}, u32[]{:S(2)}, u32[]{:S(2)}) async-start(bf16[64,304,128]{2,1,0:T(8,128)(2,1)} %shard_map.82), calls=%async_computation | async-start | bytes 9961472 | tf_op jit(solution)/shard_map/all_to_all | solution.py:197
  101.5 3.7 %copy-start.2 = (f32[4,90,16,128]{3,2,1,0:T(8,128)}, f32[4,90,16,128]{3,2,1,0:T(8,128)S(1)}, u32[]{:S(2)}) copy-start(f32[4,90,16,128]{3,2,1,0:T(8,128)S(1)} %get-tuple-element.71.field_ref) | copy-start | bytes 8847364
  101.5 4.4 %copy-start.1 = (f32[4,90,16,128]{3,2,1,0:T(8,128)}, f32[4,90,16,128]{3,2,1,0:T(8,128)S(1)}, u32[]{:S(2)}) copy-start(f32[4,90,16,128]{3,2,1,0:T(8,128)S(1)} %get-tuple-element.72.coef_ref) | copy-start | bytes 8847364
  110.3 8.0 %copy-start.14 = (f32[1,90,1,16,4]{1,0,4,3,2:T(1,128)S(1)}, f32[1,90,1,16,4]{1,0,4,3,2:T(1,128)}, u32[]{:S(2)}) copy-start(f32[1,90,1,16,4]{1,0,4,3,2:T(1,128)} %get-tuple-element.66) | copy-start | bytes 69124
  125.2 8.0 %copy-start.15 = (f32[1,90,1,16,4]{1,0,4,3,2:T(1,128)S(1)}, f32[1,90,1,16,4]{1,0,4,3,2:T(1,128)}, u32[]{:S(2)}) copy-start(f32[1,90,1,16,4]{1,0,4,3,2:T(1,128)} %get-tuple-element.58) | copy-start | bytes 69124
  213.9 13.3 %copy-start.18 = (f32[300]{0:T(512)S(1)}, f32[300]{0:T(512)}, u32[]{:S(2)}) copy-start(f32[300]{0:T(512)} %param.15) | copy-start | bytes 3604
  228.1 13.9 %collective-permute-start.9 = (bf16[300,4,128]{0,2,1:T(8,128)(2,1)S(1)}, bf16[300,4,128]{0,2,1:T(8,128)(2,1)S(1)}, u32[]{:S(2)}, u32[]{:S(2)}) collective-permute-start(bf16[300,4,128]{0,2,1:T(8,128)(2,1)S(1)} %get-tuple-element.46), channel_id=1, source_target_pairs={{0,8},{8,16},{16,24},{24,0},{1,9},{9,17},{17,25},{25,1},{2,10},{10... | collective-permute-start | bytes 921608 | tf_op jit(solution)/shard_map/ppermute | solution.py:19
  229.7 19.3 %collective-permute-start.8 = (bf16[300,4,128]{0,2,1:T(8,128)(2,1)S(1)}, bf16[300,4,128]{0,2,1:T(8,128)(2,1)S(1)}, u32[]{:S(2)}, u32[]{:S(2)}) collective-permute-start(bf16[300,4,128]{0,2,1:T(8,128)(2,1)S(1)} %get-tuple-element.45), channel_id=1, source_target_pairs={{0,24},{8,0},{16,8},{24,16},{1,25},{9,1},{17,9},{25,17},{2,26},{10... | collective-permute-start | bytes 921608 | tf_op jit(solution)/shard_map/ppermute | solution.py:20
  251.0 6.1 %copy-start.3 = (f32[45,8,16,128]{3,2,1,0:T(8,128)}, f32[45,8,16,128]{3,2,1,0:T(8,128)S(1)}, u32[]{:S(2)}) copy-start(f32[45,8,16,128]{3,2,1,0:T(8,128)S(1)} %copy.206) | copy-start | bytes 8847364
  251.0 6.1 %collective-permute-start.11 = (bf16[300,64]{0,1:T(8,128)(2,1)S(1)}, bf16[300,64]{0,1:T(8,128)(2,1)S(1)}, u32[]{:S(2)}, u32[]{:S(2)}) collective-permute-start(bf16[300,64]{0,1:T(8,128)(2,1)S(1)} %reshape.103), channel_id=1, source_target_pairs={{0,1},{1,2},{2,3},{3,4},{4,5},{5,6},{6,7},{7,0},{8,9},{9,10},{10,1... | collective-permute-start | bytes 115208 | tf_op jit(solution)/shard_map/ppermute | solution.py:30
  251.1 6.0 %collective-permute-start.10 = (bf16[300,64]{0,1:T(8,128)(2,1)S(1)}, bf16[300,64]{0,1:T(8,128)(2,1)S(1)}, u32[]{:S(2)}, u32[]{:S(2)}) collective-permute-start(bf16[300,64]{0,1:T(8,128)(2,1)S(1)} %reshape.102), channel_id=1, source_target_pairs={{0,7},{1,0},{2,1},{3,2},{4,3},{5,4},{6,5},{7,6},{8,15},{9,8},{10,9... | collective-permute-start | bytes 115208 | tf_op jit(solution)/shard_map/ppermute | solution.py:31
  257.9 10.0 %copy-start.10 = (f32[90,16,12]{2,1,0:T(8,128)S(1)}, f32[90,16,12]{2,1,0:T(8,128)}, u32[]{:S(2)}) copy-start(f32[90,16,12]{2,1,0:T(8,128)} %get-tuple-element.11) | copy-start | bytes 207364
  257.9 10.0 %copy-start.11 = (f32[90,16,12]{2,1,0:T(8,128)S(1)}, f32[90,16,12]{2,1,0:T(8,128)}, u32[]{:S(2)}) copy-start(f32[90,16,12]{2,1,0:T(8,128)} %get-tuple-element.12) | copy-start | bytes 207364
  258.0 10.0 %copy-start.12 = (f32[90,16,12]{2,1,0:T(8,128)S(1)}, f32[90,16,12]{2,1,0:T(8,128)}, u32[]{:S(2)}) copy-start(f32[90,16,12]{2,1,0:T(8,128)} %get-tuple-element.13) | copy-start | bytes 207364
  258.0 9.9 %copy-start.13 = (f32[90,16,12]{2,1,0:T(8,128)S(1)}, f32[90,16,12]{2,1,0:T(8,128)}, u32[]{:S(2)}) copy-start(f32[90,16,12]{2,1,0:T(8,128)} %get-tuple-element.14) | copy-start | bytes 207364

commit v4 on v1

--- a/solution.py
+++ b/solution.py
@@ -16,8 +16,8 @@
 
 
 def rims(core, closed):
-    north = lax.ppermute(core[:, -STEPS:], "lat", ring("lat", 1))
-    south = lax.ppermute(core[:, :STEPS], "lat", ring("lat", -1))
+    north = lax.ppermute(core[:, -STEPS:].astype(jnp.bfloat16), "lat", ring("lat", 1)).astype(core.dtype)
+    south = lax.ppermute(core[:, :STEPS].astype(jnp.bfloat16), "lat", ring("lat", -1)).astype(core.dtype)
     if closed:
         place = lax.axis_index("lat")
         zero = jnp.zeros((), core.dtype)
@@ -25,11 +25,11 @@
         south = jnp.where(place == lax.axis_size("lat") - 1, zero, south)
     main = jnp.concatenate([core, south, north], axis=1)
     planes = main.shape[0]
-    head = main[:, :, :STEPS].reshape(planes, -1)
-    tail = main[:, :, -STEPS:].reshape(planes, -1)
+    head = main[:, :, :STEPS].reshape(planes, -1).astype(jnp.bfloat16)
+    tail = main[:, :, -STEPS:].reshape(planes, -1).astype(jnp.bfloat16)
     west = lax.ppermute(tail, "lon", ring("lon", 1))
     east = lax.ppermute(head, "lon", ring("lon", -1))
-    return main, jnp.concatenate([east, west], axis=1)
+    return main, jnp.concatenate([east, west], axis=1).astype(core.dtype)
 
 
 def side_tile(side, rows, width):

time: 309 us -> 296 us (0.958)
  waiting for transfers between devices: 70.1 us -> 43.7 us
  other arithmetic: 21.5 us -> 30.8 us
  local copies, waits for them, and re-layouts: 45.7 us -> 51 us
    ppermute x6, waiting for transfers between devices: 36 us -> 15.3 us  [the longest x3 10 us: rims(): lax.ppermute(core[:, -STEPS:].astype(jnp.bfloat16), 'lat', ring('lat', 1))]
    all_to_all x1, waiting for transfers between devices: 32.8 us -> 27.5 us  [per_device(): lax.all_to_all(sent, ('lat', 'lon'), split_axis=0, concat_axis=0, tiled=T...]
    convert_element_type x0 -> x4, other arithmetic: none -> 4.05 us  [the longest x2 1.53 us: rims(): return (main, jnp.concatenate([east, west], axis=1).astype(core.dtype))]
    concatenate x3, other arithmetic: 2.3 us -> 5.81 us  [rims(): main = jnp.concatenate([core, south, north], axis=1)]
    unnamed x30 -> x36, local copies, waits for them, and re-layouts: 22.4 us -> 25.5 us
  transfers between devices with their start and end apart: 13 -> 13, of which waited for: 7 -> 4; matrix products, arithmetic and copies ran while one was open for 17% -> 23% of each run, Pallas kernels for 24% -> 25%
where the time goes in v4:
time: 296 us; the launch traced here: 294 us
  Pallas kernels  142 us (48%)
  local copies, waits for them, and re-layouts  51 us (17%)
  waiting for transfers between devices  43.7 us (15%)
  other arithmetic  30.8 us (10%)
  starting transfers between devices  24.9 us (8%)
    pallas_call x2, Pallas kernels, spread(): pl.pallas_call(spread_kernel, out_shape=jax.ShapeDtypeStruct((planes, cor...  108 us
    all_to_all x1, waiting for transfers between devices, per_device(): lax.all_to_all(sent, ('lat', 'lon'), split_axis=0, concat_axis=0, tiled=T...  27.5 us
    unnamed x36, local copies, waits for them, and re-layouts  25.5 us
    pallas_call x1, Pallas kernels, pack(): pl.pallas_call(pack_kernel, out_shape=jax.ShapeDtypeStruct((slots, height...  20.2 us
    pallas_call x1, Pallas kernels, column_sums(): pl.pallas_call(lambda *refs: gather_kernel(comps, *refs), out_shape=jax.S...  13.2 us
    concatenate x2, other arithmetic, side_tile(): return jnp.concatenate([parts[:, 0], gap, parts[:, 1]], axis=2)  12.4 us
    slice x5, local copies, waits for them, and re-layouts, rims(): head = main[:, :, :STEPS].reshape(planes, -1).astype(jnp.bfloat16)  10.9 us
    ppermute x3, waiting for transfers between devices, rims(): lax.ppermute(core[:, -STEPS:].astype(jnp.bfloat16), 'lat', ring('lat', 1))  10 us
  transfers between devices with their start and end apart: 13, of which 4 were waited for; matrix products, arithmetic and copies ran while one was open for 23% of the time, Pallas kernels for 25%

profile of v4, /device:TPU:0, one launch (start us, length us, event | category | flops | bytes accessed | tf_op | source)
XLA Modules:
  0.0 294.2 jit_solution(11468577253783849653)
XLA Ops:
  0.0 1.6 bitcast_convert_fusion.1
  1.6 1.1 fusion.18
  2.7 3.0 %collective-permute-start.1 = (bf16[360,4,128]{2,1,0:T(4,128)(2,1)}, bf16[360,4,128]{2,1,0:T(4,128)(2,1)}, u32[]{:S(2)}, u32[]{:S(2)}) collective-permute-start(bf16[360,4,128]{2,1,0:T(4,128)(2,1)} %get-tuple-element.22), channel_id=1, source_target_pairs={{0,8},{8,16},{16,24},{24,0},{1,9},{9,17},{17,25},{25,1},{2,10},{10... | collective-permute-start | bytes 1105928 | tf_op jit(solution)/shard_map/ppermute | solution.py:19
  5.7 2.0 collective-permute-start
  7.9 1.0 fusion.17
  8.9 3.8 %collective-permute-start.4 = (bf16[360,4,128]{2,1,0:T(4,128)(2,1)S(1)}, bf16[360,4,128]{2,1,0:T(4,128)(2,1)}, u32[]{:S(2)}, u32[]{:S(2)}) collective-permute-start(bf16[360,4,128]{2,1,0:T(4,128)(2,1)S(1)} %get-tuple-element.19), channel_id=1, source_target_pairs={{0,24},{8,0},{16,8},{24,16},{1,25},{9,1},{17,9},{25,17},{2,26},{10... | collective-permute-start | bytes 1105928 | tf_op jit(solution)/shard_map/ppermute | solution.py:20
  12.7 0.2 convert_reduce_fusion
  13.0 0.7 select_reduce_fusion.1.source_ref
  13.7 4.8 %copy.28.refs_0_.refs_1_ = bf16[32,128,300]{2,1,0:T(8,128)(2,1)} copy(bf16[32,128,300]{1,0,2:T(8,128)(2,1)} %param.10) | data formatting | bytes 4915200 | tf_op args[2]
  18.5 0.1 copy.27
  18.6 0.4 select_reduce_fusion
  19.0 0.6 broadcast_add_fusion
  19.6 20.2 %shard_map.82 = bf16[64,304,128]{2,1,0:T(8,128)(2,1)} custom-call(s32[64]{0:T(128)} %select_reduce_fusion.1.source_ref, bf16[32,128,300]{2,1,0:T(8,128)(2,1)} %copy.28.refs_0_.refs_1_, bf16[32,128,300]{2,1,0:T(8,128)(2,1)} %copy.28.refs_0_.refs_1_, s32[32,2,128]{2,1,0:T(2,128)} %bitcast.73), custom_call_target="tpu_custom_call" | custom-call | tf_op jit(solution)/shard_map/pallas_call | solution.py:99
  39.8 1.2 convert_element_type.49
  41.0 1.3 convert_element_type.48
  42.3 0.9 copy-done.4
  43.2 0.4 fusion.12
  43.6 2.3 fusion.15
  46.0 3.4 %copy.31 = bf16[360,16,4]{0,2,1:T(4,128)(2,1)} copy(bf16[360,16,4]{2,1,0:T(8,128)(2,1)} %get-tuple-element.16) | data formatting | bytes 92160 | tf_op jit(solution)/shard_map/slice | solution.py:29
  49.4 1.4 convert_element_type.51
  50.8 3.4 %copy.30 = bf16[360,16,4]{0,2,1:T(4,128)(2,1)} copy(bf16[360,16,4]{2,1,0:T(8,128)(2,1)} %get-tuple-element.15) | data formatting | bytes 92160 | tf_op jit(solution)/shard_map/slice | solution.py:28
  54.2 1.4 convert_element_type.50
  55.6 2.6 collective-permute-start.2
  58.3 1.1 convert_select_fusion
  59.4 1.4 convert_select_fusion.1
  60.9 0.9 copy-done.7
  61.8 0.4 fusion.11
  62.2 2.3 fusion.14
  64.5 2.8 copy.33
  67.4 2.8 copy.32
  70.3 2.7 collective-permute-start.6
  73.0 0.8 maximum_convert_fusion
  73.8 0.9 collective-permute-done.6
  74.7 0.7 maximum_convert_fusion.1
  75.4 3.8 %all-to-all-start = ((bf16[64,304,128]{2,1,0:T(8,128)(2,1)}), bf16[64,304,128]{2,1,0:T(8,128)(2,1)}, u32[]{:S(2)}, u32[]{:S(2)}) async-start(bf16[64,304,128]{2,1,0:T(8,128)(2,1)} %shard_map.82), calls=%async_computation | async-start | bytes 9961472 | tf_op jit(solution)/shard_map/all_to_all | solution.py:170
  79.3 3.4 %pad_maximum_fusion.field_ref = f32[360,16,128]{2,1,0:T(8,128)} fusion(f32[360,4,128]{2,1,0:T(4,128)} %copy-done.3, f32[360,4,128]{2,1,0:T(4,128)} %copy-done.4, f32[360,8,128]{2,1,0:T(8,128)S(1)} %bitcast.59), kind=kLoop, calls=%fused_computation | loop fusion | flops 1474560 | bytes 5898240 | tf_op jit(solution)/shard_map/concatenate | solution.py:26
  82.7 2.1 pad_maximum_fusion.1.coef_ref
  84.8 0.7 fusion.20
  85.5 2.6 copy.48
  88.1 3.1 %copy.47 = f32[360,1,16,4]{3,2,0,1:T(8,128)} copy(f32[360,1,16,4]{0,3,2,1:T(4,128)S(1)} %get-tuple-element.25) | data formatting | bytes 184320
  91.2 0.7 reshape.82
  91.9 1.0 fusion.21
  92.9 3.2 %copy.46 = f32[360,1,16,4]{3,2,0,1:T(8,128)} copy(f32[360,1,16,4]{0,3,2,1:T(4,128)S(1)} %get-tuple-element.28) | data formatting | bytes 184320
  96.0 3.2 %copy.45 = f32[360,1,16,4]{3,2,0,1:T(8,128)} copy(f32[360,1,16,4]{0,3,2,1:T(4,128)S(1)} %get-tuple-element.27) | data formatting | bytes 184320
  99.2 8.0 %pad_maximum_fusion.3 = (f32[360,16,128]{2,1,0:T(8,128)}, f32[360,16,128]{2,1,0:T(8,128)}) fusion(f32[360,16,4]{2,1,0:T(8,128)S(1)} %bitcast.62, f32[360,16,4]{2,1,0:T(8,128)} %bitcast.63, f32[128]{0:T(128)S(1)} %pad.12.clone, f32[360,16,4]{2,1,0:T(8,128)} %bitcast.64, f32[360,16,4]{2,1,0:T(8,128)} %bitcast.65), kind=kLoop, calls=%fused_computation.3 | loop fusion | flops 2949120 | bytes 6267392 | tf_op jit(solution)/shard_map/concatenate | solution.py:39
  107.2 54.1 %shard_map.84 = f32[360,8,128]{2,1,0:T(8,128)} custom-call(f32[360,16,128]{2,1,0:T(8,128)} %pad_maximum_fusion.field_ref, f32[360,16,128]{2,1,0:T(8,128)} %get-tuple-element.30.side_ref, f32[360,16,128]{2,1,0:T(8,128)} %pad_maximum_fusion.1.coef_ref, f32[360,16,128]{2,1,0:T(8,128)} %get-tuple-element.29.coef_side_ref), custom_call_target="tpu_custom_call" | custom-call | flops 58982400 | bytes 14745600 | tf_op jit(solution)/shard_map/pallas_call | solution.py:66
  161.3 1.4 convert_element_type.58
  162.7 27.5 %all-to-all-done.refs_0_ = bf16[64,304,128]{2,1,0:T(8,128)(2,1)} async-done(((bf16[64,304,128]{2,1,0:T(8,128)(2,1)}), bf16[64,304,128]{2,1,0:T(8,128)(2,1)}, u32[]{:S(2)}, u32[]{:S(2)}) %all-to-all-start) | async-done | bytes 4980768 | tf_op jit(solution)/shard_map/all_to_all | solution.py:170
  190.2 13.2 %shard_map.83 = f32[304,1024]{1,0:T(8,128)S(1)} custom-call(bf16[64,304,128]{2,1,0:T(8,128)(2,1)} %all-to-all-done.refs_0_), custom_call_target="tpu_custom_call" | custom-call | tf_op jit(solution)/shard_map/pallas_call | solution.py:137
  203.4 0.5 fusion.3
  203.9 0.4 copy.44
  204.5 3.8 %collective-permute-start.8 = (bf16[300,4,128]{0,2,1:T(8,128)(2,1)S(1)}, bf16[300,4,128]{0,2,1:T(8,128)(2,1)S(1)}, u32[]{:S(2)}, u32[]{:S(2)}) collective-permute-start(bf16[300,4,128]{0,2,1:T(8,128)(2,1)S(1)} %get-tuple-element.17), channel_id=1, source_target_pairs={{0,24},{8,0},{16,8},{24,16},{1,25},{9,1},{17,9},{25,17},{2,26},{10... | collective-permute-start | bytes 921608 | tf_op jit(solution)/shard_map/ppermute | solution.py:20
  208.3 10.0 %collective-permute-done.9 = bf16[300,4,128]{0,2,1:T(8,128)(2,1)S(1)} collective-permute-done((bf16[300,4,128]{0,2,1:T(8,128)(2,1)S(1)}, bf16[300,4,128]{0,2,1:T(8,128)(2,1)S(1)}, u32[]{:S(2)}, u32[]{:S(2)}) %collective-permute-start.9) | collective-permute-done | bytes 307232 | tf_op jit(solution)/shard_map/ppermute | solution.py:19
  218.3 5.3 %collective-permute-done.8 = bf16[300,4,128]{0,2,1:T(8,128)(2,1)S(1)} collective-permute-done((bf16[300,4,128]{0,2,1:T(8,128)(2,1)S(1)}, bf16[300,4,128]{0,2,1:T(8,128)(2,1)S(1)}, u32[]{:S(2)}, u32[]{:S(2)}) %collective-permute-start.8) | collective-permute-done | bytes 307232 | tf_op jit(solution)/shard_map/ppermute | solution.py:20
  223.6 0.3 pad_maximum_fusion.5
  224.1 2.9 collective-permute-start.10
  227.0 1.0 convolution_bitcast_fusion
  228.0 2.2 copy.52
  230.2 0.3 convolution_bitcast_fusion.1
  230.5 0.1 copy.41
  230.7 1.7 copy.50
  232.4 3.1 %copy.49 = f32[360,1,16,4]{3,2,0,1:T(8,128)} copy(f32[360,1,16,4]{0,3,2,1:T(4,128)S(1)} %get-tuple-element.23) | data formatting | bytes 184320
  235.5 4.4 %pad_maximum_fusion.4.side_ref = f32[360,16,128]{2,1,0:T(8,128)} fusion(f32[360,16,4]{2,1,0:T(8,128)S(1)} %bitcast.67, f32[360,16,4]{2,1,0:T(8,128)} %bitcast.68, f32[128]{0:T(128)S(1)} %pad.12.clone), kind=kLoop, calls=%fused_computation.4 | loop fusion | flops 1474560 | bytes 3133952 | tf_op jit(solution)/shard_map/concatenate | solution.py:39
  239.9 54.2 %shard_map.85 = f32[360,8,128]{2,1,0:T(8,128)} custom-call(f32[360,16,128]{2,1,0:T(8,128)} %bitcast.66, f32[360,16,128]{2,1,0:T(8,128)} %pad_maximum_fusion.4.side_ref, f32[360,16,128]{2,1,0:T(8,128)} %pad_maximum_fusion.1.coef_ref, f32[360,16,128]{2,1,0:T(8,128)} %get-tuple-element.29.coef_side_ref, f32[360,8,128]{2,1,0:T(8,128)} %bitcast.57), custom_call_target="tpu_custom_call" | custom-call | flops 58982400 | bytes 14745600 | tf_op jit(solution)/shard_map/pallas_call | solution.py:66
  (56 shorter events, 1.0 us)
Async XLA Ops:
  0.0 203.4 %copy-start = (bf16[360,300]{0,1:T(8,128)(2,1)S(1)}, bf16[360,300]{0,1:T(8,128)(2,1)}, u32[]{:S(2)}) copy-start(bf16[360,300]{0,1:T(8,128)(2,1)} %param.14) | copy-start | bytes 648004
  0.0 7.8 %copy-start.2 = (f32[4,90,8,128]{3,2,1,0:T(8,128)S(1)}, f32[4,90,8,128]{3,2,1,0:T(8,128)}, u32[]{:S(2)}) copy-start(f32[4,90,8,128]{3,2,1,0:T(8,128)} %param.9) | copy-start | bytes 4423684
  1.6 11.1 %copy-start.13 = (s32[32,1]{0,1:T(1,128)S(1)}, s32[32,1]{0,1:T(1,128)}, u32[]{:S(2)}) copy-start(s32[32,1]{0,1:T(1,128)} %param.11) | copy-start | bytes 388
  1.6 11.4 %copy-start.10 = (s32[32,128]{1,0:T(8,128)S(1)}, s32[32,128]{1,0:T(8,128)}, u32[]{:S(2)}) copy-start(s32[32,128]{1,0:T(8,128)} %param.12) | copy-start | bytes 49156
  1.6 11.4 %copy-start.11 = (s32[32]{0:T(128)S(1)}, s32[32]{0:T(128)}, u32[]{:S(2)}) copy-start(s32[32]{0:T(128)} %param.13) | copy-start | bytes 388
  2.7 37.0 %collective-permute-start.1 = (bf16[360,4,128]{2,1,0:T(4,128)(2,1)}, bf16[360,4,128]{2,1,0:T(4,128)(2,1)}, u32[]{:S(2)}, u32[]{:S(2)}) collective-permute-start(bf16[360,4,128]{2,1,0:T(4,128)(2,1)} %get-tuple-element.22), channel_id=1, source_target_pairs={{0,8},{8,16},{16,24},{24,0},{1,9},{9,17},{17,25},{25,1},{2,10},{10... | collective-permute-start | bytes 1105928 | tf_op jit(solution)/shard_map/ppermute | solution.py:19
  5.7 35.2 %collective-permute-start = (bf16[360,4,128]{2,1,0:T(4,128)(2,1)}, bf16[360,4,128]{2,1,0:T(4,128)(2,1)}, u32[]{:S(2)}, u32[]{:S(2)}) collective-permute-start(bf16[360,4,128]{2,1,0:T(4,128)(2,1)} %get-tuple-element.21), channel_id=1, source_target_pairs={{0,24},{8,0},{16,8},{24,16},{1,25},{9,1},{17,9},{25,17},{2,26},{10... | collective-permute-start | bytes 1105928 | tf_op jit(solution)/shard_map/ppermute | solution.py:20
  8.9 49.4 %collective-permute-start.5 = (bf16[360,4,128]{2,1,0:T(4,128)(2,1)}, bf16[360,4,128]{2,1,0:T(4,128)(2,1)}, u32[]{:S(2)}, u32[]{:S(2)}) collective-permute-start(bf16[360,4,128]{2,1,0:T(4,128)(2,1)} %get-tuple-element.20), channel_id=1, source_target_pairs={{0,8},{8,16},{16,24},{24,0},{1,9},{9,17},{17,25},{25,1},{2,10},{10... | collective-permute-start | bytes 1105928 | tf_op jit(solution)/shard_map/ppermute | solution.py:19
  8.9 50.6 %collective-permute-start.4 = (bf16[360,4,128]{2,1,0:T(4,128)(2,1)S(1)}, bf16[360,4,128]{2,1,0:T(4,128)(2,1)}, u32[]{:S(2)}, u32[]{:S(2)}) collective-permute-start(bf16[360,4,128]{2,1,0:T(4,128)(2,1)S(1)} %get-tuple-element.19), channel_id=1, source_target_pairs={{0,24},{8,0},{16,8},{24,16},{1,25},{9,1},{17,9},{25,17},{2,26},{10... | collective-permute-start | bytes 1105928 | tf_op jit(solution)/shard_map/ppermute | solution.py:20
  39.8 3.4 %copy-start.1 = (f32[4,90,8,128]{3,2,1,0:T(8,128)S(1)}, f32[4,90,8,128]{3,2,1,0:T(8,128)}, u32[]{:S(2)}) copy-start(f32[4,90,8,128]{3,2,1,0:T(8,128)} %param.8) | copy-start | bytes 4423684
  40.9 1.4 copy-start.3
  42.3 0.9 copy-start.4
  50.8 22.2 %collective-permute-start.3 = (bf16[360,64]{0,1:T(8,128)(2,1)}, bf16[360,64]{0,1:T(8,128)(2,1)}, u32[]{:S(2)}, u32[]{:S(2)}) collective-permute-start(bf16[360,64]{0,1:T(8,128)(2,1)} %convert_element_type.51), channel_id=1, source_target_pairs={{0,1},{1,2},{2,3},{3,4},{4,5},{5,6},{6,7},{7,0},{8,9},{9,10},{10,1... | collective-permute-start | bytes 138248 | tf_op jit(solution)/shard_map/ppermute | solution.py:30
  55.6 17.3 %collective-permute-start.2 = (bf16[360,64]{0,1:T(8,128)(2,1)}, bf16[360,64]{0,1:T(8,128)(2,1)}, u32[]{:S(2)}, u32[]{:S(2)}) collective-permute-start(bf16[360,64]{0,1:T(8,128)(2,1)} %convert_element_type.50), channel_id=1, source_target_pairs={{0,7},{1,0},{2,1},{3,2},{4,3},{5,4},{6,5},{7,6},{8,15},{9,8},{10,9... | collective-permute-start | bytes 138248 | tf_op jit(solution)/shard_map/ppermute | solution.py:31
  59.4 1.4 copy-start.5
  60.9 0.9 copy-start.7
  67.4 6.4 %collective-permute-start.7 = (bf16[360,64]{0,1:T(8,128)(2,1)S(1)}, bf16[360,64]{0,1:T(8,128)(2,1)S(1)}, u32[]{:S(2)}, u32[]{:S(2)}) collective-permute-start(bf16[360,64]{0,1:T(8,128)(2,1)S(1)} %convert_element_type.56), channel_id=1, source_target_pairs={{0,1},{1,2},{2,3},{3,4},{4,5},{5,6},{6,7},{7,0},{8,9},{9,10},{10,1... | collective-permute-start | bytes 138248 | tf_op jit(solution)/shard_map/ppermute | solution.py:30
  70.3 4.4 %collective-permute-start.6 = (bf16[360,64]{0,1:T(8,128)(2,1)S(1)}, bf16[360,64]{0,1:T(8,128)(2,1)S(1)}, u32[]{:S(2)}, u32[]{:S(2)}) collective-permute-start(bf16[360,64]{0,1:T(8,128)(2,1)S(1)} %convert_element_type.55), channel_id=1, source_target_pairs={{0,7},{1,0},{2,1},{3,2},{4,3},{5,4},{6,5},{7,6},{8,15},{9,8},{10,9... | collective-permute-start | bytes 138248 | tf_op jit(solution)/shard_map/ppermute | solution.py:31
  75.4 114.8 %all-to-all-start = ((bf16[64,304,128]{2,1,0:T(8,128)(2,1)}), bf16[64,304,128]{2,1,0:T(8,128)(2,1)}, u32[]{:S(2)}, u32[]{:S(2)}) async-start(bf16[64,304,128]{2,1,0:T(8,128)(2,1)} %shard_map.82), calls=%async_computation | async-start | bytes 9961472 | tf_op jit(solution)/shard_map/all_to_all | solution.py:170
  79.3 3.4 %copy-start.6 = (f32[360,4,128]{2,1,0:T(4,128)S(1)}, f32[360,4,128]{2,1,0:T(4,128)}, u32[]{:S(2)}) copy-start(f32[360,4,128]{2,1,0:T(4,128)} %copy-done.5) | copy-start | bytes 2211844
  79.3 3.4 %copy-start.8 = (f32[360,4,128]{2,1,0:T(4,128)S(1)}, f32[360,4,128]{2,1,0:T(4,128)}, u32[]{:S(2)}) copy-start(f32[360,4,128]{2,1,0:T(4,128)} %copy-done.7) | copy-start | bytes 2211844
  82.7 2.1 copy-start.9
  162.7 40.7 %copy-start.12 = (f32[300]{0:T(512)S(1)}, f32[300]{0:T(512)}, u32[]{:S(2)}) copy-start(f32[300]{0:T(512)} %param.15) | copy-start | bytes 3604
  204.4 13.9 %collective-permute-start.9 = (bf16[300,4,128]{0,2,1:T(8,128)(2,1)S(1)}, bf16[300,4,128]{0,2,1:T(8,128)(2,1)S(1)}, u32[]{:S(2)}, u32[]{:S(2)}) collective-permute-start(bf16[300,4,128]{0,2,1:T(8,128)(2,1)S(1)} %get-tuple-element.18), channel_id=1, source_target_pairs={{0,8},{8,16},{16,24},{24,0},{1,9},{9,17},{17,25},{25,1},{2,10},{10... | collective-permute-start | bytes 921608 | tf_op jit(solution)/shard_map/ppermute | solution.py:19
  204.5 19.1 %collective-permute-start.8 = (bf16[300,4,128]{0,2,1:T(8,128)(2,1)S(1)}, bf16[300,4,128]{0,2,1:T(8,128)(2,1)S(1)}, u32[]{:S(2)}, u32[]{:S(2)}) collective-permute-start(bf16[300,4,128]{0,2,1:T(8,128)(2,1)S(1)} %get-tuple-element.17), channel_id=1, source_target_pairs={{0,24},{8,0},{16,8},{24,16},{1,25},{9,1},{17,9},{25,17},{2,26},{10... | collective-permute-start | bytes 921608 | tf_op jit(solution)/shard_map/ppermute | solution.py:20
  224.0 6.2 %collective-permute-start.11 = (bf16[300,64]{0,1:T(8,128)(2,1)S(1)}, bf16[300,64]{0,1:T(8,128)(2,1)S(1)}, u32[]{:S(2)}, u32[]{:S(2)}) collective-permute-start(bf16[300,64]{0,1:T(8,128)(2,1)S(1)} %reshape.89), channel_id=1, source_target_pairs={{0,1},{1,2},{2,3},{3,4},{4,5},{5,6},{6,7},{7,0},{8,9},{9,10},{10,1... | collective-permute-start | bytes 115208 | tf_op jit(solution)/shard_map/ppermute | solution.py:30
  224.1 6.1 %collective-permute-start.10 = (bf16[300,64]{0,1:T(8,128)(2,1)S(1)}, bf16[300,64]{0,1:T(8,128)(2,1)S(1)}, u32[]{:S(2)}, u32[]{:S(2)}) collective-permute-start(bf16[300,64]{0,1:T(8,128)(2,1)S(1)} %reshape.88), channel_id=1, source_target_pairs={{0,7},{1,0},{2,1},{3,2},{4,3},{5,4},{6,5},{7,6},{8,15},{9,8},{10,9... | collective-permute-start | bytes 115208 | tf_op jit(solution)/shard_map/ppermute | solution.py:31

commit v5 on v4

--- a/solution.py
+++ b/solution.py
@@ -44,7 +44,7 @@
     core, width = out_ref.shape[1:]
     rows, lanes = field_ref.shape[1], 2 * width
 
-    @pl.loop(0, out_ref.shape[0], unroll=4)
+    @pl.loop(0, out_ref.shape[0], unroll=8)
     def _(i):
         coef = jnp.concatenate([coef_ref[i], coef_side_ref[i]], axis=1)
         field = jnp.concatenate([field_ref[i], side_ref[i]], axis=1)

time: 296 us -> 271 us (0.916)
  Pallas kernels: 142 us -> 91.7 us
  waiting for transfers between devices: 43.7 us -> 68.7 us
    pallas_call x2, Pallas kernels: 108 us -> 58.3 us  [spread(): pl.pallas_call(spread_kernel, out_shape=jax.ShapeDtypeStruct((planes, cor...]
    all_to_all x1, waiting for transfers between devices: 27.5 us -> 52.4 us  [per_device(): lax.all_to_all(sent, ('lat', 'lon'), split_axis=0, concat_axis=0, tiled=T...]
  transfers between devices with their start and end apart: 13 -> 13, of which waited for: 4 -> 4; matrix products, arithmetic and copies ran while one was open for 23% -> 25% of each run, Pallas kernels for 25% -> 18%
where the time goes in v5:
time: 271 us; the launch traced here: 269 us
  Pallas kernels  91.7 us (34%)
  waiting for transfers between devices  68.7 us (25%)
  local copies, waits for them, and re-layouts  51 us (19%)
  other arithmetic  30.8 us (11%)
  starting transfers between devices  24.9 us (9%)
    pallas_call x2, Pallas kernels, spread(): pl.pallas_call(spread_kernel, out_shape=jax.ShapeDtypeStruct((planes, cor...  58.3 us
    all_to_all x1, waiting for transfers between devices, per_device(): lax.all_to_all(sent, ('lat', 'lon'), split_axis=0, concat_axis=0, tiled=T...  52.4 us
    unnamed x36, local copies, waits for them, and re-layouts  25.5 us
    pallas_call x1, Pallas kernels, pack(): pl.pallas_call(pack_kernel, out_shape=jax.ShapeDtypeStruct((slots, height...  20.2 us
    pallas_call x1, Pallas kernels, column_sums(): pl.pallas_call(lambda *refs: gather_kernel(comps, *refs), out_shape=jax.S...  13.2 us
    concatenate x2, other arithmetic, side_tile(): return jnp.concatenate([parts[:, 0], gap, parts[:, 1]], axis=2)  12.4 us
    slice x5, local copies, waits for them, and re-layouts, rims(): head = main[:, :, :STEPS].reshape(planes, -1).astype(jnp.bfloat16)  10.9 us
    ppermute x3, waiting for transfers between devices, rims(): lax.ppermute(core[:, -STEPS:].astype(jnp.bfloat16), 'lat', ring('lat', 1))  10 us
  transfers between devices with their start and end apart: 13, of which 4 were waited for; matrix products, arithmetic and copies ran while one was open for 25% of the time, Pallas kernels for 18%

profile of v5, /device:TPU:0, one launch (start us, length us, event | category | flops | bytes accessed | tf_op | source)
XLA Modules:
  0.0 269.1 jit_solution(10859653367117298225)
XLA Ops:
  0.0 1.6 bitcast_convert_fusion.1
  1.6 1.1 fusion.18
  2.7 3.0 %collective-permute-start.1 = (bf16[360,4,128]{2,1,0:T(4,128)(2,1)}, bf16[360,4,128]{2,1,0:T(4,128)(2,1)}, u32[]{:S(2)}, u32[]{:S(2)}) collective-permute-start(bf16[360,4,128]{2,1,0:T(4,128)(2,1)} %get-tuple-element.22), channel_id=1, source_target_pairs={{0,8},{8,16},{16,24},{24,0},{1,9},{9,17},{17,25},{25,1},{2,10},{10... | collective-permute-start | bytes 1105928 | tf_op jit(solution)/shard_map/ppermute | solution.py:19
  5.7 2.0 collective-permute-start
  7.9 1.0 fusion.17
  8.9 3.8 %collective-permute-start.4 = (bf16[360,4,128]{2,1,0:T(4,128)(2,1)S(1)}, bf16[360,4,128]{2,1,0:T(4,128)(2,1)}, u32[]{:S(2)}, u32[]{:S(2)}) collective-permute-start(bf16[360,4,128]{2,1,0:T(4,128)(2,1)S(1)} %get-tuple-element.19), channel_id=1, source_target_pairs={{0,24},{8,0},{16,8},{24,16},{1,25},{9,1},{17,9},{25,17},{2,26},{10... | collective-permute-start | bytes 1105928 | tf_op jit(solution)/shard_map/ppermute | solution.py:20
  12.7 0.2 convert_reduce_fusion
  13.0 0.7 select_reduce_fusion.1.source_ref
  13.7 4.8 %copy.28.refs_0_.refs_1_ = bf16[32,128,300]{2,1,0:T(8,128)(2,1)} copy(bf16[32,128,300]{1,0,2:T(8,128)(2,1)} %param.10) | data formatting | bytes 4915200 | tf_op args[2]
  18.5 0.1 copy.27
  18.6 0.4 select_reduce_fusion
  19.0 0.6 broadcast_add_fusion
  19.6 20.2 %shard_map.82 = bf16[64,304,128]{2,1,0:T(8,128)(2,1)} custom-call(s32[64]{0:T(128)} %select_reduce_fusion.1.source_ref, bf16[32,128,300]{2,1,0:T(8,128)(2,1)} %copy.28.refs_0_.refs_1_, bf16[32,128,300]{2,1,0:T(8,128)(2,1)} %copy.28.refs_0_.refs_1_, s32[32,2,128]{2,1,0:T(2,128)} %bitcast.73), custom_call_target="tpu_custom_call" | custom-call | tf_op jit(solution)/shard_map/pallas_call | solution.py:99
  39.8 1.2 convert_element_type.49
  41.0 1.3 convert_element_type.48
  42.3 0.9 copy-done.4
  43.2 0.4 fusion.12
  43.6 2.3 fusion.15
  46.0 3.4 %copy.31 = bf16[360,16,4]{0,2,1:T(4,128)(2,1)} copy(bf16[360,16,4]{2,1,0:T(8,128)(2,1)} %get-tuple-element.16) | data formatting | bytes 92160 | tf_op jit(solution)/shard_map/slice | solution.py:29
  49.4 1.4 convert_element_type.51
  50.8 3.4 %copy.30 = bf16[360,16,4]{0,2,1:T(4,128)(2,1)} copy(bf16[360,16,4]{2,1,0:T(8,128)(2,1)} %get-tuple-element.15) | data formatting | bytes 92160 | tf_op jit(solution)/shard_map/slice | solution.py:28
  54.2 1.4 convert_element_type.50
  55.6 2.6 collective-permute-start.2
  58.3 1.1 convert_select_fusion
  59.5 1.4 convert_select_fusion.1
  60.9 0.9 copy-done.7
  61.8 0.4 fusion.11
  62.2 2.3 fusion.14
  64.6 2.8 %copy.33 = bf16[360,16,4]{0,2,1:T(4,128)(2,1)S(1)} copy(bf16[360,16,4]{2,1,0:T(8,128)(2,1)} %get-tuple-element.14) | data formatting | bytes 92160 | tf_op jit(solution)/shard_map/slice | solution.py:29
  67.5 2.8 %copy.32 = bf16[360,16,4]{0,2,1:T(4,128)(2,1)S(1)} copy(bf16[360,16,4]{2,1,0:T(8,128)(2,1)} %get-tuple-element.13) | data formatting | bytes 92160 | tf_op jit(solution)/shard_map/slice | solution.py:28
  70.3 2.7 collective-permute-start.6
  73.0 0.8 maximum_convert_fusion
  73.8 0.9 collective-permute-done.6
  74.7 0.7 maximum_convert_fusion.1
  75.4 3.8 %all-to-all-start = ((bf16[64,304,128]{2,1,0:T(8,128)(2,1)}), bf16[64,304,128]{2,1,0:T(8,128)(2,1)}, u32[]{:S(2)}, u32[]{:S(2)}) async-start(bf16[64,304,128]{2,1,0:T(8,128)(2,1)} %shard_map.82), calls=%async_computation | async-start | bytes 9961472 | tf_op jit(solution)/shard_map/all_to_all | solution.py:170
  79.3 3.4 %pad_maximum_fusion.field_ref = f32[360,16,128]{2,1,0:T(8,128)} fusion(f32[360,4,128]{2,1,0:T(4,128)} %copy-done.3, f32[360,4,128]{2,1,0:T(4,128)} %copy-done.4, f32[360,8,128]{2,1,0:T(8,128)S(1)} %bitcast.59), kind=kLoop, calls=%fused_computation | loop fusion | flops 1474560 | bytes 5898240 | tf_op jit(solution)/shard_map/concatenate | solution.py:26
  82.7 2.1 pad_maximum_fusion.1.coef_ref
  84.9 0.7 fusion.20
  85.5 2.6 copy.48
  88.1 3.1 %copy.47 = f32[360,1,16,4]{3,2,0,1:T(8,128)} copy(f32[360,1,16,4]{0,3,2,1:T(4,128)S(1)} %get-tuple-element.25) | data formatting | bytes 184320
  91.2 0.7 reshape.82
  91.9 1.0 fusion.21
  92.9 3.2 %copy.46 = f32[360,1,16,4]{3,2,0,1:T(8,128)} copy(f32[360,1,16,4]{0,3,2,1:T(4,128)S(1)} %get-tuple-element.28) | data formatting | bytes 184320
  96.0 3.2 %copy.45 = f32[360,1,16,4]{3,2,0,1:T(8,128)} copy(f32[360,1,16,4]{0,3,2,1:T(4,128)S(1)} %get-tuple-element.27) | data formatting | bytes 184320
  99.2 8.0 %pad_maximum_fusion.3 = (f32[360,16,128]{2,1,0:T(8,128)}, f32[360,16,128]{2,1,0:T(8,128)}) fusion(f32[360,16,4]{2,1,0:T(8,128)S(1)} %bitcast.62, f32[360,16,4]{2,1,0:T(8,128)} %bitcast.63, f32[128]{0:T(128)S(1)} %pad.12.clone, f32[360,16,4]{2,1,0:T(8,128)} %bitcast.64, f32[360,16,4]{2,1,0:T(8,128)} %bitcast.65), kind=kLoop, calls=%fused_computation.3 | loop fusion | flops 2949120 | bytes 6267392 | tf_op jit(solution)/shard_map/concatenate | solution.py:39
  107.2 29.1 %shard_map.84 = f32[360,8,128]{2,1,0:T(8,128)} custom-call(f32[360,16,128]{2,1,0:T(8,128)} %pad_maximum_fusion.field_ref, f32[360,16,128]{2,1,0:T(8,128)} %get-tuple-element.30.side_ref, f32[360,16,128]{2,1,0:T(8,128)} %pad_maximum_fusion.1.coef_ref, f32[360,16,128]{2,1,0:T(8,128)} %get-tuple-element.29.coef_side_ref), custom_call_target="tpu_custom_call" | custom-call | flops 58982400 | bytes 14745600 | tf_op jit(solution)/shard_map/pallas_call | solution.py:66
  136.3 1.4 convert_element_type.58
  137.8 52.4 %all-to-all-done.refs_0_ = bf16[64,304,128]{2,1,0:T(8,128)(2,1)} async-done(((bf16[64,304,128]{2,1,0:T(8,128)(2,1)}), bf16[64,304,128]{2,1,0:T(8,128)(2,1)}, u32[]{:S(2)}, u32[]{:S(2)}) %all-to-all-start) | async-done | bytes 4980768 | tf_op jit(solution)/shard_map/all_to_all | solution.py:170
  190.2 13.2 %shard_map.83 = f32[304,1024]{1,0:T(8,128)S(1)} custom-call(bf16[64,304,128]{2,1,0:T(8,128)(2,1)} %all-to-all-done.refs_0_), custom_call_target="tpu_custom_call" | custom-call | tf_op jit(solution)/shard_map/pallas_call | solution.py:137
  203.4 0.5 fusion.3
  203.9 0.4 copy.44
  204.5 3.8 %collective-permute-start.8 = (bf16[300,4,128]{0,2,1:T(8,128)(2,1)S(1)}, bf16[300,4,128]{0,2,1:T(8,128)(2,1)S(1)}, u32[]{:S(2)}, u32[]{:S(2)}) collective-permute-start(bf16[300,4,128]{0,2,1:T(8,128)(2,1)S(1)} %get-tuple-element.17), channel_id=1, source_target_pairs={{0,24},{8,0},{16,8},{24,16},{1,25},{9,1},{17,9},{25,17},{2,26},{10... | collective-permute-start | bytes 921608 | tf_op jit(solution)/shard_map/ppermute | solution.py:20
  208.3 10.0 %collective-permute-done.9 = bf16[300,4,128]{0,2,1:T(8,128)(2,1)S(1)} collective-permute-done((bf16[300,4,128]{0,2,1:T(8,128)(2,1)S(1)}, bf16[300,4,128]{0,2,1:T(8,128)(2,1)S(1)}, u32[]{:S(2)}, u32[]{:S(2)}) %collective-permute-start.9) | collective-permute-done | bytes 307232 | tf_op jit(solution)/shard_map/ppermute | solution.py:19
  218.3 5.3 %collective-permute-done.8 = bf16[300,4,128]{0,2,1:T(8,128)(2,1)S(1)} collective-permute-done((bf16[300,4,128]{0,2,1:T(8,128)(2,1)S(1)}, bf16[300,4,128]{0,2,1:T(8,128)(2,1)S(1)}, u32[]{:S(2)}, u32[]{:S(2)}) %collective-permute-start.8) | collective-permute-done | bytes 307232 | tf_op jit(solution)/shard_map/ppermute | solution.py:20
  223.6 0.3 pad_maximum_fusion.5
  224.1 2.9 %collective-permute-start.10 = (bf16[300,64]{0,1:T(8,128)(2,1)S(1)}, bf16[300,64]{0,1:T(8,128)(2,1)S(1)}, u32[]{:S(2)}, u32[]{:S(2)}) collective-permute-start(bf16[300,64]{0,1:T(8,128)(2,1)S(1)} %reshape.88), channel_id=1, source_target_pairs={{0,7},{1,0},{2,1},{3,2},{4,3},{5,4},{6,5},{7,6},{8,15},{9,8},{10,9... | collective-permute-start | bytes 115208 | tf_op jit(solution)/shard_map/ppermute | solution.py:31
  227.0 1.0 convolution_bitcast_fusion
  228.0 2.2 copy.52
  230.1 0.3 convolution_bitcast_fusion.1
  230.5 0.1 copy.41
  230.7 1.7 copy.50
  232.4 3.1 %copy.49 = f32[360,1,16,4]{3,2,0,1:T(8,128)} copy(f32[360,1,16,4]{0,3,2,1:T(4,128)S(1)} %get-tuple-element.23) | data formatting | bytes 184320
  235.5 4.4 %pad_maximum_fusion.4.side_ref = f32[360,16,128]{2,1,0:T(8,128)} fusion(f32[360,16,4]{2,1,0:T(8,128)S(1)} %bitcast.67, f32[360,16,4]{2,1,0:T(8,128)} %bitcast.68, f32[128]{0:T(128)S(1)} %pad.12.clone), kind=kLoop, calls=%fused_computation.4 | loop fusion | flops 1474560 | bytes 3133952 | tf_op jit(solution)/shard_map/concatenate | solution.py:39
  239.9 29.2 %shard_map.85 = f32[360,8,128]{2,1,0:T(8,128)} custom-call(f32[360,16,128]{2,1,0:T(8,128)} %bitcast.66, f32[360,16,128]{2,1,0:T(8,128)} %pad_maximum_fusion.4.side_ref, f32[360,16,128]{2,1,0:T(8,128)} %pad_maximum_fusion.1.coef_ref, f32[360,16,128]{2,1,0:T(8,128)} %get-tuple-element.29.coef_side_ref, f32[360,8,128]{2,1,0:T(8,128)} %bitcast.57), custom_call_target="tpu_custom_call" | custom-call | flops 58982400 | bytes 14745600 | tf_op jit(solution)/shard_map/pallas_call | solution.py:66
  (56 shorter events, 1.0 us)
Async XLA Ops:
  0.0 203.4 %copy-start = (bf16[360,300]{0,1:T(8,128)(2,1)S(1)}, bf16[360,300]{0,1:T(8,128)(2,1)}, u32[]{:S(2)}) copy-start(bf16[360,300]{0,1:T(8,128)(2,1)} %param.14) | copy-start | bytes 648004
  0.0 7.8 %copy-start.2 = (f32[4,90,8,128]{3,2,1,0:T(8,128)S(1)}, f32[4,90,8,128]{3,2,1,0:T(8,128)}, u32[]{:S(2)}) copy-start(f32[4,90,8,128]{3,2,1,0:T(8,128)} %param.9) | copy-start | bytes 4423684
  1.6 11.1 %copy-start.13 = (s32[32,1]{0,1:T(1,128)S(1)}, s32[32,1]{0,1:T(1,128)}, u32[]{:S(2)}) copy-start(s32[32,1]{0,1:T(1,128)} %param.11) | copy-start | bytes 388
  1.6 11.4 %copy-start.10 = (s32[32,128]{1,0:T(8,128)S(1)}, s32[32,128]{1,0:T(8,128)}, u32[]{:S(2)}) copy-start(s32[32,128]{1,0:T(8,128)} %param.12) | copy-start | bytes 49156
  1.6 11.4 %copy-start.11 = (s32[32]{0:T(128)S(1)}, s32[32]{0:T(128)}, u32[]{:S(2)}) copy-start(s32[32]{0:T(128)} %param.13) | copy-start | bytes 388
  2.7 37.1 %collective-permute-start.1 = (bf16[360,4,128]{2,1,0:T(4,128)(2,1)}, bf16[360,4,128]{2,1,0:T(4,128)(2,1)}, u32[]{:S(2)}, u32[]{:S(2)}) collective-permute-start(bf16[360,4,128]{2,1,0:T(4,128)(2,1)} %get-tuple-element.22), channel_id=1, source_target_pairs={{0,8},{8,16},{16,24},{24,0},{1,9},{9,17},{17,25},{25,1},{2,10},{10... | collective-permute-start | bytes 1105928 | tf_op jit(solution)/shard_map/ppermute | solution.py:19
  5.7 35.2 %collective-permute-start = (bf16[360,4,128]{2,1,0:T(4,128)(2,1)}, bf16[360,4,128]{2,1,0:T(4,128)(2,1)}, u32[]{:S(2)}, u32[]{:S(2)}) collective-permute-start(bf16[360,4,128]{2,1,0:T(4,128)(2,1)} %get-tuple-element.21), channel_id=1, source_target_pairs={{0,24},{8,0},{16,8},{24,16},{1,25},{9,1},{17,9},{25,17},{2,26},{10... | collective-permute-start | bytes 1105928 | tf_op jit(solution)/shard_map/ppermute | solution.py:20
  8.9 49.4 %collective-permute-start.5 = (bf16[360,4,128]{2,1,0:T(4,128)(2,1)}, bf16[360,4,128]{2,1,0:T(4,128)(2,1)}, u32[]{:S(2)}, u32[]{:S(2)}) collective-permute-start(bf16[360,4,128]{2,1,0:T(4,128)(2,1)} %get-tuple-element.20), channel_id=1, source_target_pairs={{0,8},{8,16},{16,24},{24,0},{1,9},{9,17},{17,25},{25,1},{2,10},{10... | collective-permute-start | bytes 1105928 | tf_op jit(solution)/shard_map/ppermute | solution.py:19
  8.9 50.6 %collective-permute-start.4 = (bf16[360,4,128]{2,1,0:T(4,128)(2,1)S(1)}, bf16[360,4,128]{2,1,0:T(4,128)(2,1)}, u32[]{:S(2)}, u32[]{:S(2)}) collective-permute-start(bf16[360,4,128]{2,1,0:T(4,128)(2,1)S(1)} %get-tuple-element.19), channel_id=1, source_target_pairs={{0,24},{8,0},{16,8},{24,16},{1,25},{9,1},{17,9},{25,17},{2,26},{10... | collective-permute-start | bytes 1105928 | tf_op jit(solution)/shard_map/ppermute | solution.py:20
  39.8 3.4 %copy-start.1 = (f32[4,90,8,128]{3,2,1,0:T(8,128)S(1)}, f32[4,90,8,128]{3,2,1,0:T(8,128)}, u32[]{:S(2)}) copy-start(f32[4,90,8,128]{3,2,1,0:T(8,128)} %param.8) | copy-start | bytes 4423684
  41.0 1.4 copy-start.3
  42.3 0.9 copy-start.4
  50.8 22.2 %collective-permute-start.3 = (bf16[360,64]{0,1:T(8,128)(2,1)}, bf16[360,64]{0,1:T(8,128)(2,1)}, u32[]{:S(2)}, u32[]{:S(2)}) collective-permute-start(bf16[360,64]{0,1:T(8,128)(2,1)} %convert_element_type.51), channel_id=1, source_target_pairs={{0,1},{1,2},{2,3},{3,4},{4,5},{5,6},{6,7},{7,0},{8,9},{9,10},{10,1... | collective-permute-start | bytes 138248 | tf_op jit(solution)/shard_map/ppermute | solution.py:30
  55.6 17.3 %collective-permute-start.2 = (bf16[360,64]{0,1:T(8,128)(2,1)}, bf16[360,64]{0,1:T(8,128)(2,1)}, u32[]{:S(2)}, u32[]{:S(2)}) collective-permute-start(bf16[360,64]{0,1:T(8,128)(2,1)} %convert_element_type.50), channel_id=1, source_target_pairs={{0,7},{1,0},{2,1},{3,2},{4,3},{5,4},{6,5},{7,6},{8,15},{9,8},{10,9... | collective-permute-start | bytes 138248 | tf_op jit(solution)/shard_map/ppermute | solution.py:31
  59.4 1.4 copy-start.5
  60.9 0.9 copy-start.7
  67.4 6.4 %collective-permute-start.7 = (bf16[360,64]{0,1:T(8,128)(2,1)S(1)}, bf16[360,64]{0,1:T(8,128)(2,1)S(1)}, u32[]{:S(2)}, u32[]{:S(2)}) collective-permute-start(bf16[360,64]{0,1:T(8,128)(2,1)S(1)} %convert_element_type.56), channel_id=1, source_target_pairs={{0,1},{1,2},{2,3},{3,4},{4,5},{5,6},{6,7},{7,0},{8,9},{9,10},{10,1... | collective-permute-start | bytes 138248 | tf_op jit(solution)/shard_map/ppermute | solution.py:30
  70.3 4.4 %collective-permute-start.6 = (bf16[360,64]{0,1:T(8,128)(2,1)S(1)}, bf16[360,64]{0,1:T(8,128)(2,1)S(1)}, u32[]{:S(2)}, u32[]{:S(2)}) collective-permute-start(bf16[360,64]{0,1:T(8,128)(2,1)S(1)} %convert_element_type.55), channel_id=1, source_target_pairs={{0,7},{1,0},{2,1},{3,2},{4,3},{5,4},{6,5},{7,6},{8,15},{9,8},{10,9... | collective-permute-start | bytes 138248 | tf_op jit(solution)/shard_map/ppermute | solution.py:31
  75.4 114.8 %all-to-all-start = ((bf16[64,304,128]{2,1,0:T(8,128)(2,1)}), bf16[64,304,128]{2,1,0:T(8,128)(2,1)}, u32[]{:S(2)}, u32[]{:S(2)}) async-start(bf16[64,304,128]{2,1,0:T(8,128)(2,1)} %shard_map.82), calls=%async_computation | async-start | bytes 9961472 | tf_op jit(solution)/shard_map/all_to_all | solution.py:170
  79.3 3.4 %copy-start.6 = (f32[360,4,128]{2,1,0:T(4,128)S(1)}, f32[360,4,128]{2,1,0:T(4,128)}, u32[]{:S(2)}) copy-start(f32[360,4,128]{2,1,0:T(4,128)} %copy-done.5) | copy-start | bytes 2211844
  79.3 3.4 %copy-start.8 = (f32[360,4,128]{2,1,0:T(4,128)S(1)}, f32[360,4,128]{2,1,0:T(4,128)}, u32[]{:S(2)}) copy-start(f32[360,4,128]{2,1,0:T(4,128)} %copy-done.7) | copy-start | bytes 2211844
  82.7 2.1 copy-start.9
  137.7 65.7 %copy-start.12 = (f32[300]{0:T(512)S(1)}, f32[300]{0:T(512)}, u32[]{:S(2)}) copy-start(f32[300]{0:T(512)} %param.15) | copy-start | bytes 3604
  204.4 13.9 %collective-permute-start.9 = (bf16[300,4,128]{0,2,1:T(8,128)(2,1)S(1)}, bf16[300,4,128]{0,2,1:T(8,128)(2,1)S(1)}, u32[]{:S(2)}, u32[]{:S(2)}) collective-permute-start(bf16[300,4,128]{0,2,1:T(8,128)(2,1)S(1)} %get-tuple-element.18), channel_id=1, source_target_pairs={{0,8},{8,16},{16,24},{24,0},{1,9},{9,17},{17,25},{25,1},{2,10},{10... | collective-permute-start | bytes 921608 | tf_op jit(solution)/shard_map/ppermute | solution.py:19
  204.5 19.1 %collective-permute-start.8 = (bf16[300,4,128]{0,2,1:T(8,128)(2,1)S(1)}, bf16[300,4,128]{0,2,1:T(8,128)(2,1)S(1)}, u32[]{:S(2)}, u32[]{:S(2)}) collective-permute-start(bf16[300,4,128]{0,2,1:T(8,128)(2,1)S(1)} %get-tuple-element.17), channel_id=1, source_target_pairs={{0,24},{8,0},{16,8},{24,16},{1,25},{9,1},{17,9},{25,17},{2,26},{10... | collective-permute-start | bytes 921608 | tf_op jit(solution)/shard_map/ppermute | solution.py:20
  224.0 6.2 %collective-permute-start.11 = (bf16[300,64]{0,1:T(8,128)(2,1)S(1)}, bf16[300,64]{0,1:T(8,128)(2,1)S(1)}, u32[]{:S(2)}, u32[]{:S(2)}) collective-permute-start(bf16[300,64]{0,1:T(8,128)(2,1)S(1)} %reshape.89), channel_id=1, source_target_pairs={{0,1},{1,2},{2,3},{3,4},{4,5},{5,6},{6,7},{7,0},{8,9},{9,10},{10,1... | collective-permute-start | bytes 115208 | tf_op jit(solution)/shard_map/ppermute | solution.py:30
  224.1 6.1 %collective-permute-start.10 = (bf16[300,64]{0,1:T(8,128)(2,1)S(1)}, bf16[300,64]{0,1:T(8,128)(2,1)S(1)}, u32[]{:S(2)}, u32[]{:S(2)}) collective-permute-start(bf16[300,64]{0,1:T(8,128)(2,1)S(1)} %reshape.88), channel_id=1, source_target_pairs={{0,7},{1,0},{2,1},{3,2},{4,3},{5,4},{6,5},{7,6},{8,15},{9,8},{10,9... | collective-permute-start | bytes 115208 | tf_op jit(solution)/shard_map/ppermute | solution.py:31
